TPU v7x, 32 devices: a whole 2x2x4 slice. The times are simulated.
32 devices in a mesh: stream: 2 (over core), blk: 16 (over z, y, x).
Axes of the slice: x: 2, y: 2, z: 4, core: 2. Of those that a mesh axis runs over, the one named last changes fastest.
Arguments:
- inputs: bfloat16 [2, 2, 2048, 1536], P(None, 'stream', 'blk'), may hold values from -6 to 6
- cotangent: bfloat16 [2, 2, 2048, 1536], P(None, 'stream', 'blk'), may hold values from -6 to 6
- seq_lengths: int32 [2, 2, 9], P(None, 'stream'), may hold values from 1 to 1984, as said below
- gain_attn: bfloat16 [1536], P(('stream', 'blk')), may hold values from 0.5 to 1.5
- gain_ffn: bfloat16 [1536], P(('stream', 'blk')), may hold values from 0.5 to 1.5
- w_query: bfloat16 [1536, 1536], P(('stream', 'blk')), may hold values from -0.15625 to 0.15625
- w_key: bfloat16 [1536, 768], P(('stream', 'blk')), may hold values from -0.15625 to 0.15625
- w_value: bfloat16 [1536, 768], P(('stream', 'blk')), may hold values from -0.15625 to 0.15625
- w_out: bfloat16 [1536, 1536], P(('stream', 'blk')), may hold values from -0.625 to 0.625
- w_gate: bfloat16 [1536, 4096], P(('stream', 'blk')), may hold values from -0.15625 to 0.15625
- w_up: bfloat16 [1536, 4096], P(('stream', 'blk')), may hold values from -0.15625 to 0.15625
- w_down: bfloat16 [4096, 1536], P(('stream', 'blk')), may hold values from -0.09375 to 0.09375
Outputs:
- output: bfloat16 [2, 2, 2048, 1536], P(None, 'stream', 'blk')
- input_grad: float32 [2, 2, 2048, 1536], P(None, 'stream', 'blk')
- grad_gain_attn: float32 [1536], P(('stream', 'blk'))
- grad_gain_ffn: float32 [1536], P(('stream', 'blk'))
- grad_w_query: float32 [1536, 1536], P(('stream', 'blk'))
- grad_w_key: float32 [1536, 768], P(('stream', 'blk'))
- grad_w_value: float32 [1536, 768], P(('stream', 'blk'))
- grad_w_out: float32 [1536, 1536], P(('stream', 'blk'))
- grad_w_gate: float32 [1536, 4096], P(('stream', 'blk'))
- grad_w_up: float32 [1536, 4096], P(('stream', 'blk'))
- grad_w_down: float32 [4096, 1536], P(('stream', 'blk'))
Inputs may be any that keep to these rules, and one draw needn't show every extreme that they name: `seq_lengths`: the lengths of a pack sum to 2048; one sequence of each pack, at a place drawn from the seed, is the longest. In the packs of even-numbered micro-batches each other sequence holds at most (127) // 8 positions and together they hold a fixed number. In the packs of odd-numbered micro-batches each other sequence holds 64 to 192 positions and the longest holds exactly 1024.
All inputs are finite; a program needn't handle non-finite values.
Results may differ from a plain program's by a relative error of at most 0.019.
Values may be sent and summed in bfloat16 or wider, within the bound.
No kernel may reach another device: no remote copies, remote signals or barrier semaphores. Data moves between devices by JAX's collectives and lax.ppermute only.
A program may use at most 640 MiB of HBM per device.

v0:
```python
import math

import jax
import jax.numpy as jnp
import numpy as np
from jax import lax
from jax.experimental import pallas as pl
from jax.experimental.pallas import tpu as pltpu
from jax.sharding import Mesh
from jax.sharding import PartitionSpec as P

HQ = 16
HK = 8
DH = 96
PLANE = 4
FF_TILES = 2
LANES = 128
VMEM_BYTES = 50 * 1024 * 1024

epsilon = 1e-05
rope_base = 100000.0
masked_score = -1e30
score_scale = 1.0 / math.sqrt(DH)
exp2_scale = score_scale * math.log2(math.e)

LIGHT = pl.CostEstimate(flops=1, bytes_accessed=1, transcendentals=0)
CHUNK_COST = pl.CostEstimate(flops=1, bytes_accessed=6000000, transcendentals=0)

f32 = jnp.float32
bf16 = jnp.bfloat16


def spread(heads):
    table = np.zeros((heads * DH, heads * LANES), np.float32)
    for head in range(heads):
        for i in range(DH):
            lane = i if i < DH // 2 else i + (LANES - DH) // 2
            table[head * DH + i, head * LANES + lane] = 1.0
    return jnp.asarray(table, bf16)


def rms_scale(values):
    return lax.rsqrt(jnp.mean(values * values, axis=-1, keepdims=True) + epsilon)


def dot(a, b):
    return jnp.dot(a, b, preferred_element_type=f32)


def dot_nt(a, b):
    return lax.dot_general(a, b, (((1,), (1,)), ((), ())), preferred_element_type=f32)


def dot_tn(a, b):
    return lax.dot_general(a, b, (((0,), (0,)), ((), ())), preferred_element_type=f32)


def project_kernel(size, info_ref, x_ref, cos_ref, sin_ref, e4_ref, e8_ref, *rest):
    blocks, (n_ref, q_ref, kv_ref, w_ref, out_w_ref, gains_ref, scale_ref, pad_s) = rest[: 2 * size], rest[2 * size :]
    rows = blocks[0].shape[0]
    heads = 8 * DH

    @pl.when(pl.program_id(0) == 0)
    def _():
        for i, block in enumerate(blocks):
            core = info_ref[1] if i < size else 1 - info_ref[1]
            start = pl.multiple_of((core * size + lax.rem(info_ref[0] - i % size + size, size)) * rows, rows)
            w_ref[pl.ds(start, rows), :] = block[:, : heads + LANES]
            out_w_ref[pl.ds(start, rows), :] = block[:, heads + LANES :]
            pad_s[pl.ds(start, rows), :] = dot(block[:, :heads], e8_ref[...]).astype(bf16)
        rows_to = lax.broadcasted_iota(jnp.int32, (LANES, LANES), 0)
        same = (rows_to == lax.broadcasted_iota(jnp.int32, (LANES, LANES), 1)).astype(bf16)
        gains_ref[...] = dot_nt(same[:8], w_ref[:, heads:])

    x = x_ref[...].astype(f32)
    scale = rms_scale(x)
    scale_ref[...] = scale
    normed = (x * scale * gains_ref[0:1, :]).astype(bf16)
    n_ref[...] = normed
    pre = dot(normed, pad_s[...])
    cos, sin = cos_ref[...], sin_ref[...]
    parts = []
    for head in range(8):
        piece = pre[:, head * LANES : (head + 1) * LANES]
        if head < 6:
            piece = piece * cos + pltpu.roll(piece, LANES // 2, 1) * sin
        parts.append(piece.astype(bf16))
    q_ref[...] = jnp.concatenate(parts[:4], axis=1)
    kv_ref[...] = dot_nt(jnp.concatenate(parts[4:], axis=1), e4_ref[...]).astype(bf16)


def project(info, x, blocks, cos, sin, e4, e8):
    rows, width = x.shape
    step = min(256, rows)
    size = len(blocks) // 2
    cols = blocks[0].shape[1]
    first = 8 * DH + LANES
    whole = lambda a: pl.BlockSpec(a.shape, lambda i, n: (0,) * a.ndim)
    by_row = lambda c: pl.BlockSpec((step, c), lambda i, n: (i, 0))
    return pl.pallas_call(
        lambda *refs: project_kernel(size, *refs),
        grid_spec=pltpu.PrefetchScalarGridSpec(
            num_scalar_prefetch=1,
            grid=(rows // step,),
            in_specs=[by_row(width), by_row(LANES), by_row(LANES), whole(e4), whole(e8)] + [whole(b) for b in blocks],
            out_specs=[
                by_row(width),
                by_row(4 * LANES),
                by_row(4 * DH),
                pl.BlockSpec((width, first), lambda i, n: (0, 0)),
                pl.BlockSpec((width, cols - first), lambda i, n: (0, 0)),
                pl.BlockSpec((8, width), lambda i, n: (0, 0)),
                by_row(1),
            ],
            scratch_shapes=[pltpu.VMEM((width, 8 * LANES), bf16)],
        ),
        out_shape=[
            jax.ShapeDtypeStruct((rows, width), bf16),
            jax.ShapeDtypeStruct((rows, 4 * LANES), bf16),
            jax.ShapeDtypeStruct((rows, 4 * DH), bf16),
            jax.ShapeDtypeStruct((width, first), bf16),
            jax.ShapeDtypeStruct((width, cols - first), bf16),
            jax.ShapeDtypeStruct((8, width), f32),
            jax.ShapeDtypeStruct((rows, 1), f32),
        ],
        compiler_params=pltpu.CompilerParams(vmem_limit_bytes=VMEM_BYTES),
        cost_estimate=LIGHT,
        name="project",
    )(info, x, cos, sin, e4, e8, *blocks)


def assemble_kernel(size, info_ref, *rest):
    blocks, out_ref = rest[: 2 * size], rest[2 * size]
    rows = blocks[0].shape[0]
    for i, block in enumerate(blocks):
        core = info_ref[1] if i < size else 1 - info_ref[1]
        start = pl.multiple_of((core * size + lax.rem(info_ref[0] - i % size + size, size)) * rows, rows)
        out_ref[pl.ds(start, rows), :] = block[...]


def assemble(info, blocks):
    size = len(blocks) // 2
    rows, width = blocks[0].shape
    step = width // 3 if width % 384 == 0 else width // 4
    return pl.pallas_call(
        lambda *refs: assemble_kernel(size, *refs),
        grid_spec=pltpu.PrefetchScalarGridSpec(
            num_scalar_prefetch=1,
            grid=(width // step,),
            in_specs=[pl.BlockSpec((rows, step), lambda i, n: (0, i)) for _ in blocks],
            out_specs=pl.BlockSpec((len(blocks) * rows, step), lambda i, n: (0, i)),
        ),
        out_shape=jax.ShapeDtypeStruct((len(blocks) * rows, width), blocks[0].dtype),
        compiler_params=pltpu.CompilerParams(vmem_limit_bytes=VMEM_BYTES),
        cost_estimate=LIGHT,
        name="assemble",
    )(info, *blocks)


def allowed_of(info_ref, k, chunk, qpos_ref, qbeg_ref, kpos_ref):
    kpos = kpos_ref[...] + (info_ref[0] - k) * chunk
    return (kpos <= qpos_ref[...]) & (kpos >= qbeg_ref[...])


def useful_of(info_ref, m, k, chunk):
    z = info_ref[0]
    return (k <= z) & ((z - k + 1) * chunk - 1 >= info_ref[2 + m])


def stack_heads(block, h):
    return jnp.concatenate(
        [block[:, (2 * h) * LANES : (2 * h + 1) * LANES], block[:, (2 * h + 1) * LANES : (2 * h + 2) * LANES]], axis=0
    )


def run_kernel(body, info, inputs, outs, aliases, name):
    def spec(entry):
        if isinstance(entry, tuple):
            return pl.BlockSpec(entry[1], lambda i, n: entry[2])
        return pl.BlockSpec(entry.shape, lambda i, n: (0,) * entry.ndim)

    return list(
        pl.pallas_call(
            body,
            grid_spec=pltpu.PrefetchScalarGridSpec(
                num_scalar_prefetch=1,
                grid=(1,),
                in_specs=[spec(entry) for entry in inputs],
                out_specs=[pl.BlockSpec(o.shape, lambda i, n, o=o: (0,) * len(o.shape)) for o in outs],
            ),
            out_shape=outs,
            input_output_aliases=aliases,
            compiler_params=pltpu.CompilerParams(vmem_limit_bytes=VMEM_BYTES),
            cost_estimate=CHUNK_COST,
            name=name,
        )(info, *[entry[0] if isinstance(entry, tuple) else entry for entry in inputs])
    )


def attend_kernel(m, k, last, info_ref, q_ref, kv_ref, qpos_ref, qbeg_ref, kpos_ref, e_ref, *rest):
    chunk = kv_ref.shape[0]
    if k > 0:
        top_in, acc_in, rest = rest[0], rest[1], rest[2:]
    top_ref, acc_ref = rest[0], rest[1]

    def run():
        allowed = allowed_of(info_ref, k, chunk, qpos_ref, qbeg_ref, kpos_ref)
        kv = kv_ref[...]
        q = q_ref[...]
        one_lane = (lax.broadcasted_iota(jnp.int32, (1, LANES), 1) == DH // 2).astype(f32)
        for h in range(2):
            keys = dot(kv, e_ref[:, h * LANES : (h + 1) * LANES]).astype(bf16)
            vals = (dot(kv, e_ref[:, (2 + h) * LANES : (3 + h) * LANES]) + one_lane).astype(bf16)
            s = jnp.where(allowed, dot_nt(keys, stack_heads(q, h)), masked_score)
            new = jnp.max(s, axis=0, keepdims=True)
            if k > 0:
                old = top_in[h]
                new = jnp.maximum(old, new)
            w = jnp.where(allowed, jnp.exp2((s - new) * exp2_scale), 0.0).astype(bf16)
            acc = dot_tn(vals, w)
            if k > 0:
                acc = acc_in[h] * jnp.exp2((old - new) * exp2_scale) + acc
            acc_ref[h] = acc
            top_ref[h] = new

    if k == 0:
        run()
    else:
        useful = useful_of(info_ref, m, k, chunk)
        pl.when(useful)(run)

        @pl.when(jnp.logical_not(useful))
        def _():
            top_ref[...] = top_in[...]
            acc_ref[...] = acc_in[...]

    if last:
        att_ref, low_ref, lse_ref = rest[2:]
        parts = []
        for h in range(2):
            acc = acc_ref[h]
            total = acc[DH // 2 : DH // 2 + 1, :]
            lse_ref[h] = top_ref[h] * exp2_scale + jnp.log2(total)
            flat = (acc / total).T
            rows = flat.shape[0] // 2
            parts += [flat[:rows], flat[rows:]]
        att = jnp.concatenate(parts, axis=1)
        att_ref[...] = att
        low_ref[...] = dot_nt(att.astype(bf16), e_ref[...]).astype(bf16)


def attend(m, k, last, info, q, kv, qpos, qbeg, kpos, e4, state):
    rows = q[1][0]
    outs = [jax.ShapeDtypeStruct((2, 1, 2 * rows), f32), jax.ShapeDtypeStruct((2, LANES, 2 * rows), f32)]
    if last:
        outs += [
            jax.ShapeDtypeStruct((rows, 4 * LANES), f32),
            jax.ShapeDtypeStruct((rows, 4 * DH), bf16),
            jax.ShapeDtypeStruct((2, 1, 2 * rows), f32),
        ]
    return run_kernel(
        lambda *refs: attend_kernel(m, k, last, *refs),
        info,
        [q, kv, qpos, qbeg, kpos, e4] + state,
        outs,
        {7: 0, 8: 1} if k > 0 else {},
        "attend",
    )


def attend_back_kernel(
    m, k, first, last, info_ref, q_ref, kv_ref, lse_ref, qpos_ref, qbeg_ref, kpos_ref, cosk_ref, sink_ref, e_ref, *rest
):
    chunk = kv_ref.shape[0]
    if first:
        g_ref, att_ref, rest = rest[0], rest[1], rest[2:]
        go_ref, delta_ref, dq_ref, dkv_ref = rest[:4]
        go = dot(g_ref[...], e_ref[...])
        for h in range(2):
            go_h = stack_heads(go, h)
            go_ref[h] = go_h.astype(bf16)
            prod = go_h * stack_heads(att_ref[...], h)
            delta_ref[h] = jnp.sum(prod.T, axis=0, keepdims=True)
    else:
        go_ref, delta_ref, dq_in, moved_ref, rest = rest[0], rest[1], rest[2], rest[3], rest[4:]
        dq_ref, dkv_ref = rest[:2]

    def run():
        allowed = allowed_of(info_ref, k, chunk, qpos_ref, qbeg_ref, kpos_ref)
        kv = kv_ref[...]
        q = q_ref[...]
        cosk, sink = cosk_ref[...], sink_ref[...]
        grad_keys, grad_vals = [], []
        for h in range(2):
            keys = dot(kv, e_ref[:, h * LANES : (h + 1) * LANES]).astype(bf16)
            vals = dot(kv, e_ref[:, (2 + h) * LANES : (3 + h) * LANES]).astype(bf16)
            q_h = stack_heads(q, h)
            go_h = go_ref[h]
            s = dot_nt(keys, q_h)
            w = jnp.where(allowed, jnp.exp2(s * exp2_scale - lse_ref[h]), 0.0)
            grad_vals.append(dot(w.astype(bf16), go_h).astype(bf16))
            ds = (w * (dot_nt(vals, go_h) - delta_ref[h])).astype(bf16)
            dq = dot_tn(keys, ds)
            dq_ref[h] = dq if first else dq_in[h] + dq
            gk = dot(ds, q_h) * score_scale
            gk = gk * cosk + pltpu.roll(gk * sink, LANES // 2, 1)
            grad_keys.append(gk.astype(bf16))
        total = dot_nt(jnp.concatenate(grad_keys + grad_vals, axis=1), e_ref[...])
        if not first:
            total = total + moved_ref[...].astype(f32)
        dkv_ref[...] = total.astype(bf16)

    if k == 0:
        run()
    else:
        useful = useful_of(info_ref, m, k, chunk)
        pl.when(useful)(run)

        @pl.when(jnp.logical_not(useful))
        def _():
            dkv_ref[...] = jnp.zeros(dkv_ref.shape, bf16) if first else moved_ref[...]
            dq_ref[...] = jnp.zeros(dq_ref.shape, f32) if first else dq_in[...]

    if last:
        out_ref = rest[-1]
        parts = []
        for h in range(2):
            flat = dq_ref[h].T * score_scale
            rows = flat.shape[0] // 2
            for piece in (flat[:rows], flat[rows:]):
                parts.append((piece * cosk_ref[...] + pltpu.roll(piece * sink_ref[...], LANES // 2, 1)).astype(bf16))
        out_ref[...] = dot_nt(jnp.concatenate(parts, axis=1), e_ref[...]).astype(bf16)


def attend_back(m, k, first, last, info, q, kv, lse, qpos, qbeg, kpos, cosk, sink, e4, state):
    rows = q[1][0]
    outs = []
    if first:
        outs += [jax.ShapeDtypeStruct((2, 2 * rows, LANES), bf16), jax.ShapeDtypeStruct((2, 1, 2 * rows), f32)]
    outs += [jax.ShapeDtypeStruct((2, LANES, 2 * rows), f32), jax.ShapeDtypeStruct((rows, 4 * DH), bf16)]
    if last:
        outs += [jax.ShapeDtypeStruct((rows, 4 * DH), bf16)]
    return run_kernel(
        lambda *refs: attend_back_kernel(m, k, first, last, *refs),
        info,
        [q, kv, lse, qpos, qbeg, kpos, cosk, sink, e4] + state,
        outs,
        {} if first else {12: 0},
        "attend_back",
    )


def store_split(sum_of, tok_rows, first_ref, second_ref, keep_first_ref, keep_second_ref):
    for i, slot in enumerate((1, 3)):
        first_ref[i] = sum_of(slot * tok_rows, tok_rows).astype(bf16)
        keep_first_ref[i] = sum_of((slot - 1) * tok_rows, tok_rows)
    for i in range(2):
        second_ref[i] = sum_of((PLANE + 2 + i) * tok_rows, tok_rows).astype(bf16)
        keep_second_ref[i] = sum_of((PLANE + i) * tok_rows, tok_rows)


def split_outs(tok_rows, width):
    return [jax.ShapeDtypeStruct((2, tok_rows, width), kind) for kind in (bf16, bf16, f32, f32)]


def dot_split_kernel(tok_rows, a_ref, w_ref, *rest):
    acc_s = rest[-1]
    acc_s[...] = dot(a_ref[...], w_ref[...])
    store_split(lambda start, n: acc_s[start : start + n, :], tok_rows, *rest[:-1])


def dot_split(a, w):
    rows, inner = a.shape
    tok_rows = rows // (2 * PLANE)
    width = w.shape[1]
    step = width // 3
    outs = split_outs(tok_rows, width)
    return list(
        pl.pallas_call(
            lambda *refs: dot_split_kernel(tok_rows, *refs),
            grid=(3,),
            in_specs=[pl.BlockSpec((rows, inner), lambda i: (0, 0)), pl.BlockSpec((inner, step), lambda i: (0, i))],
            out_specs=[pl.BlockSpec((2, tok_rows, step), lambda i: (0, 0, i)) for _ in outs],
            out_shape=outs,
            scratch_shapes=[pltpu.VMEM((rows, step), f32)],
            compiler_params=pltpu.CompilerParams(vmem_limit_bytes=VMEM_BYTES),
            cost_estimate=LIGHT,
            name="dot_split",
        )(a, w)
    )


def ffn_kernel(size, tok_rows, info_ref, n_ref, g_ref, *rest):
    gu_blocks, down_blocks, rest = rest[: 2 * size], rest[2 * size : 4 * size], rest[4 * size :]
    hidden_ref, *outs = rest[:5]
    gu_theirs_ref, gu_mine_ref, down_theirs_ref, down_mine_ref = rest[5:9]
    gu_s, down_s, acc_s, flat_s, grad_s = rest[9:]
    f, last = pl.program_id(0), pl.num_programs(0) - 1
    units = hidden_ref.shape[1]
    half = flat_s.shape[0] // 2

    def place(i, rows):
        core = info_ref[1] if i < size else 1 - info_ref[1]
        return pl.ds(pl.multiple_of((core * size + lax.rem(info_ref[0] - i % size + size, size)) * rows, rows), rows)

    @pl.when(f == 0)
    def _():
        acc_s[...] = jnp.zeros(acc_s.shape, f32)
        flat_s[...] = n_ref[...].T
        for i, block in enumerate(down_blocks):
            down_s[place(i, block.shape[0]), :] = block[...]

    for i, block in enumerate(gu_blocks):
        gu_s[place(i, block.shape[0]), :] = block[...]
    w_down = down_s.at[pl.ds(pl.multiple_of(f * units, units), units)]
    step = 4 * tok_rows

    @pl.loop(0, n_ref.shape[0] // step)
    def _(r):
        at = pl.ds(pl.multiple_of(r * step, step), step)
        pre = dot(n_ref[at, :], gu_s[...])
        grad_hidden = dot_nt(g_ref[at, :], w_down[...])
        gate_pre, up_pre = pre[:, :units], pre[:, units:]
        sigmoid_gate = jax.nn.sigmoid(gate_pre)
        silu_gate = gate_pre * sigmoid_gate
        hidden_ref[at, :] = (silu_gate * up_pre).astype(bf16)
        grad_gate = grad_hidden * up_pre * sigmoid_gate * (1.0 + gate_pre * (1.0 - sigmoid_gate))
        both = jnp.concatenate([grad_gate.astype(bf16), (grad_hidden * silu_gate).astype(bf16)], axis=1)
        grad_s[at, :] = both
        acc_s[at, :] += dot_nt(both, gu_s[...])

    core = info_ref[1]
    gu_mine_ref[...] = dot(flat_s[pl.ds(pl.multiple_of(core * half, half), half), :], grad_s[...]).astype(bf16)
    gu_theirs_ref[...] = dot(flat_s[pl.ds(pl.multiple_of((1 - core) * half, half), half), :], grad_s[...]).astype(bf16)
    term_down = dot_tn(hidden_ref[...], g_ref[...]).astype(bf16)
    is_mine = lax.div(f, pl.num_programs(0) // 2) == core

    @pl.when(is_mine)
    def _():
        down_mine_ref[...] = term_down

    @pl.when(jnp.logical_not(is_mine))
    def _():
        down_theirs_ref[...] = term_down

    @pl.when(f == last)
    def _():
        store_split(lambda start, n: acc_s[start : start + n, :], tok_rows, *outs)


def ffn(info, normed, grad_mlp, gu_blocks, down_blocks):
    rows, width = normed.shape
    size = len(gu_blocks) // 2
    tok_rows = rows // (2 * PLANE)
    ff_part = gu_blocks[0].shape[1] // 2
    units = ff_part // FF_TILES
    whole = lambda a: pl.BlockSpec(a.shape, lambda f, n: (0,) * a.ndim, pipeline_mode=pl.Buffered(1))
    outs = split_outs(tok_rows, width)
    gu_half = pl.BlockSpec((width // 2, 2 * units), lambda f, n: (0, f))

    def down_half(core_of):
        return pl.BlockSpec((units, width), lambda f, n: (jnp.clip(f - core_of(n) * (FF_TILES // 2), 0, FF_TILES // 2 - 1), 0))

    return list(
        pl.pallas_call(
            lambda *refs: ffn_kernel(size, tok_rows, *refs),
            grid_spec=pltpu.PrefetchScalarGridSpec(
                num_scalar_prefetch=1,
                grid=(FF_TILES,),
                in_specs=[whole(normed), whole(grad_mlp)]
                + [pl.BlockSpec((block.shape[0], 2 * units), lambda f, n: (0, f)) for block in gu_blocks]
                + [whole(block) for block in down_blocks],
                out_specs=[pl.BlockSpec((rows, units), lambda f, n: (0, f))]
                + [pl.BlockSpec(o.shape, lambda f, n: (0, 0, 0), pipeline_mode=pl.Buffered(1)) for o in outs]
                + [gu_half, gu_half, down_half(lambda n: 1 - n[1]), down_half(lambda n: n[1])],
                scratch_shapes=[
                    pltpu.VMEM((width, 2 * units), bf16),
                    pltpu.VMEM((ff_part, width), bf16),
                    pltpu.VMEM((rows, width), f32),
                    pltpu.VMEM((width, rows), bf16),
                    pltpu.VMEM((rows, 2 * units), bf16),
                ],
            ),
            out_shape=[jax.ShapeDtypeStruct((rows, ff_part), bf16)]
            + outs
            + [jax.ShapeDtypeStruct((width // 2, 2 * ff_part), bf16)] * 2
            + [jax.ShapeDtypeStruct((ff_part // 2, width), bf16)] * 2,
            compiler_params=pltpu.CompilerParams(vmem_limit_bytes=58 * 1024 * 1024),
            cost_estimate=LIGHT,
            name="ffn",
        )(info, normed, grad_mlp, *gu_blocks, *down_blocks)
    )


def project_back_kernel(tok_rows, info_ref, g_ref, w_ref, n_ref, x_ref, scale_ref, *rest):
    first_ref, second_ref, keep_first_ref, keep_second_ref, gain_ref, theirs_ref, mine_ref, acc_s = rest
    rows = 2 * tok_rows
    total = jnp.zeros((1, acc_s.shape[1]), f32)
    for i in range(g_ref.shape[0] // rows):
        at = slice(i * rows, (i + 1) * rows)
        acc = dot_nt(g_ref[at, :], w_ref[...])
        acc_s[at, :] = acc
        total = total + jnp.sum(acc * x_ref[at, :].astype(f32) * scale_ref[at, :], axis=0, keepdims=True)
    gain_ref[...] = jnp.broadcast_to(total, gain_ref.shape)
    store_split(lambda start, n: acc_s[start : start + n, :], tok_rows, first_ref, second_ref, keep_first_ref, keep_second_ref)
    term = dot_tn(n_ref[...], g_ref[...]).astype(bf16)
    is_mine = pl.program_id(0) == info_ref[1]

    @pl.when(is_mine)
    def _():
        mine_ref[...] = term

    @pl.when(jnp.logical_not(is_mine))
    def _():
        theirs_ref[...] = term


def project_back(info, grads, w, normed, x, scale):
    rows, inner = grads.shape
    tok_rows = rows // (2 * PLANE)
    width = w.shape[0]
    half = width // 2
    outs = split_outs(tok_rows, width)
    column = pl.BlockSpec((rows, half), lambda i, n: (0, i))
    out_whole = pl.BlockSpec((half, inner), lambda i, n: (0, 0))
    return list(
        pl.pallas_call(
            lambda *refs: project_back_kernel(tok_rows, *refs),
            grid_spec=pltpu.PrefetchScalarGridSpec(
                num_scalar_prefetch=1,
                grid=(2,),
                in_specs=[
                    pl.BlockSpec((rows, inner), lambda i, n: (0, 0)),
                    pl.BlockSpec((half, inner), lambda i, n: (i, 0)),
                    column,
                    column,
                    pl.BlockSpec((rows, 1), lambda i, n: (0, 0)),
                ],
                out_specs=[pl.BlockSpec((2, tok_rows, half), lambda i, n: (0, 0, i)) for _ in outs]
                + [pl.BlockSpec((8, half), lambda i, n: (0, i)), out_whole, out_whole],
                scratch_shapes=[pltpu.VMEM((rows, half), f32)],
            ),
            out_shape=outs
            + [jax.ShapeDtypeStruct((8, width), f32)]
            + [jax.ShapeDtypeStruct((half, inner), bf16)] * 2,
            compiler_params=pltpu.CompilerParams(vmem_limit_bytes=VMEM_BYTES),
            cost_estimate=LIGHT,
            name="project_back",
        )(info, grads, w, normed, x, scale)
    )


def beside(value, bit):
    return lax.ppermute(value, "plane", [(i, i ^ bit) for i in range(PLANE)])


def other_core(value):
    return lax.ppermute(value, "stream", [(0, 1), (1, 0)])


def along(value, step, wrap):
    size = lax.axis_size("zed")
    pairs = [(i, (i + step) % size) for i in range(size) if wrap or 0 <= i + step < size]
    return lax.ppermute(value, "zed", pairs)


def plane_gather_start(own):
    return [own[0], own[1], beside(own[0], 1), beside(own[1], 2)]


def plane_gather_more(first, second, first_got, second_got):
    pair_one, pair_two = jnp.stack([first, first_got]), jnp.stack([second, second_got])
    return [pair_one, pair_two, beside(pair_one, 2), beside(pair_two, 1)]


def plane_gather_end(pair_one, pair_two, first_more, second_more):
    blocks = [pair_one, first_more, pair_two[:1], second_more[:1], pair_two[1:], second_more[1:]]
    return jnp.concatenate(blocks).reshape(-1, pair_one.shape[-1])


def plane_sum_start(split):
    return [beside(split[0], 1), beside(split[1], 2)]


def plane_sum_more(split, got_first, got_second):
    keep_first, keep_second = split[2], split[3]
    more_first = beside((keep_first[1] + got_first[1]).astype(bf16), 2)
    more_second = beside((keep_second[1] + got_second[1]).astype(bf16), 1)
    return [got_first[0], got_second[0], more_first, more_second]


def plane_sum_end(split, got_first, got_second, more_first, more_second):
    return jnp.stack([split[2][0] + got_first + more_first, split[3][0] + got_second + more_second])


def after(value, *earlier):
    return lax.optimization_barrier((value,) + earlier)[0]


def sync(*values):
    return list(lax.optimization_barrier(values))


def core_halves(full):
    size = lax.axis_size("zed")
    s = lax.axis_index("stream")
    full = full.reshape((2, size, -1) + full.shape[1:])
    mine = lax.dynamic_index_in_dim(full, s, 0, keepdims=False)
    theirs = lax.dynamic_index_in_dim(full, 1 - s, 0, keepdims=False)
    return mine, other_core(theirs)


def core_sum(mine, other):
    return (mine.astype(f32) + other.astype(f32)).astype(bf16)


def ring_part(half, k):
    size = lax.axis_size("zed")
    z = lax.axis_index("zed")
    return lax.dynamic_index_in_dim(half, lax.rem(z - k + size, size), 0, keepdims=False)


def ring_add(half, moved, k):
    return (moved.astype(f32) + ring_part(half, k).astype(f32)).astype(bf16)


def plane_swap(value, split, concat):
    return lax.all_to_all(value, "plane", split_axis=split, concat_axis=concat, tiled=True)


def on_device(inputs, cotangent, seq_lengths, gain_attn, gain_ffn, w_query, w_key, w_value, w_out, w_gate, w_up, w_down):
    size = lax.axis_size("zed")
    s, z, p = lax.axis_index("stream"), lax.axis_index("zed"), lax.axis_index("plane")
    micro, _, tok_rows, width = inputs.shape
    chunk = PLANE * tok_rows
    tokens = micro * chunk
    shard_rows = w_query.shape[0]
    ff_block = w_down.shape[0]
    ff_blocks = 2 * size
    ff_part = ff_blocks * ff_block
    q_part, kv_part = HQ * DH // PLANE, HK * DH // PLANE
    out_part = width // PLANE
    e4, e8 = spread(4), spread(8)

    def by_part(weight):
        return weight.reshape(shard_rows, PLANE, -1)

    def by_ff_part(weight):
        return weight.reshape(shard_rows, ff_blocks, PLANE, ff_block).transpose(0, 2, 1, 3).reshape(shard_rows, PLANE, -1)

    def from_ff_parts(term):
        return term.reshape(shard_rows, PLANE, ff_blocks, ff_block).transpose(0, 2, 1, 3).reshape(shard_rows, -1)

    own_in = inputs[:, 0]
    own_cot = cotangent[:, 0]
    gains = jnp.stack([gain_attn, gain_ffn], axis=1)
    gains = jnp.broadcast_to(jnp.pad(gains, ((0, 0), (0, LANES - 2)))[:, None], (shard_rows, PLANE, LANES))
    qkv_bundle = jnp.concatenate([by_part(w_query), by_part(w_key), by_part(w_value), gains, by_part(w_out)], axis=2)
    qkv_block = plane_swap(qkv_bundle.reshape(shard_rows, -1), 1, 0)
    tiled = (shard_rows, PLANE, FF_TILES, ff_part // FF_TILES)
    ffn_bundle = jnp.stack([by_ff_part(w_gate).reshape(tiled), by_ff_part(w_up).reshape(tiled)], axis=3).reshape(shard_rows, -1)
    qkv_blocks = [qkv_block]
    for _ in range(size - 1):
        qkv_blocks.append(along(qkv_blocks[-1], 1, True))
    qkv_other = [other_core(block) for block in qkv_blocks]
    ffn_block = plane_swap(after(ffn_bundle, qkv_block), 1, 0)
    pieces = sync(*plane_gather_start(after(own_in, qkv_block)))
    gathered_in = plane_gather_end(*sync(*plane_gather_more(*pieces)))
    gu_blocks = [after(ffn_block, qkv_blocks[-1])]
    gu_blocks.append(along(gu_blocks[0], 1, True))

    slot_place = ((jnp.arange(PLANE, dtype=jnp.int32) ^ p)[:, None] * tok_rows + jnp.arange(tok_rows, dtype=jnp.int32)[None, :]).reshape(chunk)
    chunk_place = (z - jnp.arange(size, dtype=jnp.int32))[:, None] * chunk + slot_place[None, :]
    lengths = seq_lengths[:, 0]
    seq_ends = jnp.cumsum(lengths, axis=1)
    begins = jnp.sum(
        jnp.where(seq_ends[:, None, None, :] <= chunk_place[None, :, :, None], lengths[:, None, None, :], 0), axis=-1
    )
    own_begin = begins[:, 0]
    lane = np.arange(LANES)
    place_in_half = lane % (LANES // 2)
    real = place_in_half < DH // 2
    frequency = jnp.where(
        real, rope_base ** (-2.0 * jnp.asarray(np.minimum(place_in_half, DH // 2 - 1), f32) / DH), 0.0
    )
    rope_place = (chunk_place[None] - begins).astype(f32)

    def tables(place):
        angles = jnp.maximum(place, 0.0)[..., None] * frequency
        signs = jnp.asarray(np.where(real, np.where(lane < LANES // 2, -1.0, 1.0), 0.0), f32)
        return jnp.where(real, jnp.cos(angles), 0.0), jnp.sin(angles) * signs

    cos, sin = tables(after(rope_place[:, 0], qkv_block))
    index = jnp.stack([z, s]).astype(jnp.int32)
    info = jnp.concatenate([index, jnp.min(own_begin, axis=1)])
    qpos = jnp.tile(chunk_place[0], 2)[None]
    qbeg = jnp.tile(own_begin, (1, 2))[:, None]
    kpos = slot_place[:, None]

    normed_one, q_rot, kv_own, full_qkv, full_oc, full_gains, in_scale = project(
        index, gathered_in, qkv_blocks + qkv_other, cos.reshape(tokens, LANES), sin.reshape(tokens, LANES), e4, e8
    )
    full_qkv = full_qkv[:, : q_part + 2 * kv_part]
    gain_one, gain_two = full_gains[0:1], full_gains[1:2]
    full_out = plane_swap(full_oc, 0, 1)
    cot_pieces = plane_gather_start(after(own_cot, gathered_in, kv_own))
    q_rot = [(q_rot, (chunk, 4 * LANES), (m, 0)) for m in range(micro)]
    kv_windows = [[(kv_own, (chunk, 4 * DH), (m, 0))] for m in range(micro)]
    kv_pieces = [[piece] for piece in kv_own.reshape(micro, chunk, 4 * DH)]
    qbeg = [(qbeg, (None, 1, 2 * chunk), (m, 0, 0)) for m in range(micro)]
    states = [[] for _ in range(micro)]
    for k in range(size):
        if k < size - 1:
            arrived = [along(kv_pieces[m][k], 1, False) for m in range(micro)]
        for m in range(micro):
            states[m] = attend(m, k, k == size - 1, info, q_rot[m], kv_windows[m][k], qpos, qbeg[m], kpos, e4, states[m])
        if k < size - 1:
            tops = [state[0] for state in states]
            if k == 0:
                tops[0], tops[1], arrived[0], arrived[1], gu_blocks[1], *cot_pieces = sync(
                    *tops, *arrived, gu_blocks[1], *cot_pieces
                )
                cot_pieces = plane_gather_more(*cot_pieces)
            elif k == 1:
                tops[0], tops[1], arrived[0], arrived[1], full_out, *cot_pieces = sync(*tops, *arrived, full_out, *cot_pieces)
            else:
                tops[0], tops[1], arrived[0], arrived[1] = sync(*tops, *arrived)
            for m in range(micro):
                states[m] = [tops[m], states[m][1]]
                kv_pieces[m].append(arrived[m])
                kv_windows[m].append(arrived[m])
    kv_there = [pieces[-1] for pieces in kv_pieces]
    attended, lse = [state[2] for state in states], [state[4] for state in states]
    attn_low = jnp.concatenate([state[3] for state in states], axis=0)
    gathered_cot = plane_gather_end(*cot_pieces)

    gu_blocks[1], down_block, rope_place = sync(gu_blocks[1], w_down, rope_place, *kv_there)[:3]
    down_blocks = [down_block, along(down_block, 1, True)]
    branch_split = dot_split(attn_low, full_out)
    branch_split = sync(*branch_split, down_blocks[1])
    down_blocks[1] = branch_split.pop()
    gu_blocks.append(along(after(gu_blocks[1], down_blocks[1]), 1, True))
    *got, gu_blocks[2] = sync(*plane_sum_start(branch_split), gu_blocks[2])
    down_blocks.append(along(after(down_blocks[1], gu_blocks[2]), 1, True))
    cos_all, sin_all = tables(after(rope_place, gu_blocks[2]))
    *got, down_blocks[2], cos_all, sin_all = sync(*plane_sum_more(branch_split, *got), down_blocks[2], cos_all, sin_all)
    layer_in = own_in.astype(f32)
    middle = layer_in + plane_sum_end(branch_split, *got)
    scale_two = rms_scale(middle)
    pieces = plane_gather_start((middle * scale_two * gain_two).astype(bf16))
    for k in range(2, size - 1):
        down_blocks.append(along(down_blocks[k], 1, True))
    *pieces, down_blocks[-1] = sync(*pieces, down_blocks[-1])
    for k in range(2, size - 1):
        gu_blocks.append(along(after(gu_blocks[k], down_blocks[-1]), 1, True))
    *pieces, gu_blocks[-1] = sync(*plane_gather_more(*pieces), gu_blocks[-1])
    normed_two = plane_gather_end(*pieces)

    gu_all = gu_blocks + [other_core(block) for block in gu_blocks]
    down_all = down_blocks + [other_core(block) for block in down_blocks]
    hidden, *outs = ffn(index, normed_two, gathered_cot, gu_all, down_all)
    normed_split, (gu_theirs, gu_mine, down_theirs, down_mine) = outs[:4], outs[4:]
    got = plane_sum_start(normed_split)
    gu_half = core_sum(gu_mine, other_core(gu_theirs)).reshape(size, -1, 2 * ff_part)
    down_half = core_sum(down_mine, other_core(down_theirs)).reshape(size, -1, width)
    gu_total, down_total = ring_part(gu_half, size - 1), ring_part(down_half, size - 1)
    *got, gu_total, down_total = sync(*got, gu_total, down_total)
    gu_moved, down_moved = along(gu_total, -1, True), along(down_total, -1, True)
    got = sync(*plane_sum_more(normed_split, *got))
    grad_normed_two = plane_sum_end(normed_split, *got)
    grad_y = own_cot.astype(f32)
    grad_gain_two = jnp.sum(grad_normed_two * middle * scale_two, axis=(0, 1))
    weighted = grad_normed_two * gain_two
    grad_middle = (
        grad_y
        + scale_two * weighted
        - middle * scale_two**3 * jnp.mean(middle * weighted, axis=-1, keepdims=True)
    )
    pieces = plane_gather_start(grad_middle.astype(bf16))
    *pieces, gu_moved, down_moved = sync(*pieces, gu_moved, down_moved)
    gu_total, down_total = ring_add(gu_half, gu_moved, size - 2), ring_add(down_half, down_moved, size - 2)
    gu_moved, down_moved = along(gu_total, -1, True), along(down_total, -1, True)
    full_down = assemble(index, [after(down_all[0], gu_total)] + down_all[1:])
    result_split = dot_split(after(hidden, gu_total), full_down)
    pieces = plane_gather_more(*pieces)
    for k in range(size - 3, -1, -1):
        gu_total, down_total = ring_add(gu_half, gu_moved, k), ring_add(down_half, down_moved, k)
        if k == size - 3:
            *pieces, gu_total, down_total, result_split[0] = sync(*pieces, gu_total, down_total, result_split[0])
        if k > 0:
            gu_moved, down_moved = along(gu_total, -1, True), along(down_total, -1, True)
    sum_gu, sum_down = gu_total, down_total
    grad_branch = plane_gather_end(*pieces)
    grad_attn = dot_nt(grad_branch, full_out).astype(bf16)

    attended[-1] = after(attended[-1], sum_down)
    states = [[(grad_attn, (chunk, q_part), (m, 0)), attended[m]] for m in range(micro)]
    grad_query = [None] * micro
    terms = [None] * micro
    for k in range(size - 1, -1, -1):
        first = k == size - 1
        for m in range(micro):
            outs = attend_back(
                m, k, first, k == 0, info, q_rot[m], kv_windows[m][k], lse[m], qpos, qbeg[m], kpos,
                (cos_all, (None, None, chunk, LANES), (m, k, 0, 0)), (sin_all, (None, None, chunk, LANES), (m, k, 0, 0)),
                e4, states[m] if first else states[m] + [moved[m]],
            )
            states[m] = outs[:3] if first else states[m][:2] + [outs[0]]
            terms[m] = outs[3] if first else outs[1]
            if k == 0:
                grad_query[m] = outs[-1]
        if k > 0:
            moved = [along(term, -1, False) for term in terms]
            moved[0] = after(moved[0], terms[-1], *([sum_gu, sum_down] if first else []))
        if first:
            got = plane_sum_start(sync(*result_split[:2], *terms)[:2])
            term_out = plane_swap(dot_tn(attn_low, after(grad_branch, *terms)).astype(bf16), 1, 0)
        elif k == size - 2:
            moved[-1], term_out, *got = sync(moved[-1], term_out, *got)
            out_mine, out_other = core_halves(term_out)
            got = plane_sum_more(result_split, *got)
        elif k == size - 3:
            moved[-1], out_other, *got = sync(moved[-1], out_other, *got)
            output = (middle + plane_sum_end(result_split, *got)).astype(bf16)
            out_half = core_sum(out_mine, out_other)

    grad_qkv = jnp.concatenate([jnp.concatenate(grad_query, axis=0), jnp.concatenate(terms, axis=0)], axis=1)
    *part_split, gain_rows, qkv_theirs, qkv_mine = project_back(index, grad_qkv, full_qkv, normed_one, gathered_in, in_scale)
    got = plane_sum_start(part_split)
    gain_terms = jnp.stack([gain_rows[0], grad_gain_two]).astype(bf16)
    gain_terms = jnp.pad(gain_terms, ((0, LANES - 2), (0, 0))).T
    gain_mine, gain_other = core_halves(gain_terms)
    qkv_half = core_sum(qkv_mine, other_core(qkv_theirs)).reshape(size, shard_rows * PLANE, -1)
    last_half = jnp.concatenate([qkv_half, out_half, core_sum(gain_mine, gain_other)], axis=-1)
    last_total = ring_part(last_half, size - 1)
    sum_gu = plane_swap(after(sum_gu, last_total), 0, 1)
    for k in range(size - 2, -1, -1):
        last_moved = along(last_total, -1, True)
        if k == size - 2:
            *got, last_moved = sync(*got, last_moved)
            got = plane_sum_more(part_split, *got)
        elif k == size - 3:
            *got, last_moved, sum_gu = sync(*got, last_moved, sum_gu)
        last_total = ring_add(last_half, last_moved, k)
    grad_normed_one = plane_sum_end(part_split, *got)
    last_total = plane_swap(last_total, 0, 1).astype(f32).reshape(shard_rows, PLANE, -1)
    scale_one = rms_scale(layer_in)
    weighted = grad_normed_one * gain_one
    input_grad = (
        grad_middle
        + scale_one * weighted
        - layer_in * scale_one**3 * jnp.mean(layer_in * weighted, axis=-1, keepdims=True)
    )
    sum_gu = sum_gu.astype(f32).reshape(shard_rows, PLANE, FF_TILES, 2, ff_part // FF_TILES)
    cuts = np.cumsum([q_part, kv_part, kv_part, out_part])
    sum_query, sum_key, sum_value, sum_out, gain_sum = jnp.split(last_total, cuts, axis=2)
    gain_sum = jnp.sum(gain_sum, axis=1)
    return (
        output[:, None],
        input_grad[:, None],
        gain_sum[:, 0],
        gain_sum[:, 1],
        sum_query.reshape(shard_rows, -1),
        sum_key.reshape(shard_rows, -1),
        sum_value.reshape(shard_rows, -1),
        sum_out.reshape(shard_rows, -1),
        from_ff_parts(sum_gu[:, :, :, 0]),
        from_ff_parts(sum_gu[:, :, :, 1]),
        sum_down.astype(f32),
    )


def solution(mesh):
    blocks = mesh.shape["blk"]
    grid = Mesh(mesh.devices.reshape(2, blocks // PLANE, PLANE), ("stream", "zed", "plane"))
    tokens = P(None, "stream", ("zed", "plane"), None)
    vector = P(("stream", "zed", "plane"))
    matrix = P(("stream", "zed", "plane"), None)
    return jax.shard_map(
        on_device,
        mesh=grid,
        in_specs=(tokens, tokens, P(None, "stream", None), vector, vector) + (matrix,) * 7,
        out_specs=(tokens, tokens, vector, vector) + (matrix,) * 7,
        check_vma=False,
    )
```

profile of v0, /device:TPU:0, one launch (start us, length us, event | category | flops | bytes accessed | tf_op | source)
XLA Modules:
  0.0 564.5 jit_solution(15765983703490358517)
XLA Ops:
  5.5 5.3 all-to-all-start
  12.1 6.4 %all-to-all-done = bf16[48,4,1280]{2,0,1:T(8,128)(2,1)S(1)} async-done(((bf16[48,4,1280]{2,0,1:T(8,128)(2,1)}), bf16[48,4,1280]{2,0,1:T(8,128)(2,1)S(1)}, u32[]{:S(2)}, u32[]{:S(2)}) %all-to-all-start) | async-done | bytes 491552 | tf_op jit(solution)/shard_map/all_to_all | solution.py:628
  59.6 5.0 collective-permute-done.6.refs_9_
  68.4 12.9 %project.1 = (bf16[1024,1536]{1,0:T(8,128)(2,1)}, bf16[1024,512]{1,0:T(8,128)(2,1)}, bf16[1024,384]{1,0:T(8,128)(2,1)}, bf16[1536,896]{1,0:T(8,128)(2,1)}, bf16[...) custom-call(s32[2]{0:T(128)S(1)} %pad_add_fusion.1.refs_0_, ...), custom_call_target="tpu_custom_call" | custom-call | flops 1 | bytes 1 | tf_op jit(solution)/shard_map/project/pallas_call | solution.py:100
  128.5 5.5 collective-permute-done.17.refs_2_
  133.9 5.0 collective-permute-done.19
  152.1 6.4 %collective-permute-done.21.refs_2_ = bf16[512,384]{1,0:T(8,128)(2,1)S(1)} collective-permute-done((bf16[512,384]{1,0:T(8,128)(2,1)}, bf16[512,384]{1,0:T(8,128)(2,1)S(1)}, u32[]{:S(2)}, u32[]{:S(2)}) %collective-permute-start.21) | collective-permute-done | bytes 393248 | tf_op jit(solution)/shard_map/ppermute | solution.py:564
  177.8 16.4 %collective-permute-done.25.refs_5_ = bf16[192,2048]{1,0:T(8,128)(2,1)S(1)} collective-permute-done((bf16[192,2048]{1,0:T(8,128)(2,1)}, bf16[192,2048]{1,0:T(8,128)(2,1)S(1)}, u32[]{:S(2)}, u32[]{:S(2)}) %collective-permute-start.25) | collective-permute-done | bytes 786464 | tf_op jit(solution)/shard_map/ppermute | solution.py:564
  196.5 9.0 %fusion.1 = (f32[2,4,512,128]{3,2,1,0:T(8,128)}, f32[2,4,512,128]{3,2,1,0:T(8,128)}) fusion(f32[128]{0:T(128)S(1)} %copy-done.145, f32[128]{0:T(128)S(1)} %copy-done.143, f32[2,4,512]{2,1,0:T(4,128)S(1)} %broadcast_maximum_fusion, pred[128]{0:T(512)(128)(4,1)S(1)} %copy-done.147), kind=kLoop, calls=%fused_computation.10 | loop fusion | flops 1572864 | bytes 4211840 | tf_op jit(solution)/shard_map/mul | solution.py:691
  215.0 7.6 %collective-permute-done.31.refs_14_.refs_4_ = bf16[128,1536]{1,0:T(8,128)(2,1)S(1)} collective-permute-done((bf16[128,1536]{1,0:T(8,128)(2,1)S(1)}, bf16[128,1536]{1,0:T(8,128)(2,1)S(1)}, u32[]{:S(2)}, u32[]{:S(2)}) %collective-permute-start.31) | collective-permute-done | bytes 393248 | tf_op jit(solution)/shard_map/ppermute | solution.py:564
  227.2 12.5 %collective-permute-done.33 = bf16[2,128,1536]{2,1,0:T(8,128)(2,1)S(1)} collective-permute-done((bf16[2,128,1536]{2,1,0:T(8,128)(2,1)S(1)}, bf16[2,128,1536]{2,1,0:T(8,128)(2,1)S(1)}, u32[]{:S(2)}, u32[]{:S(2)}) %collective-permute-start.33) | collective-permute-done | bytes 786464 | tf_op jit(solution)/shard_map/ppermute | solution.py:554
  248.2 41.0 %ffn.1 = (bf16[1024,1024]{1,0:T(8,128)(2,1)}, bf16[2,128,1536]{2,1,0:T(8,128)(2,1)}, bf16[2,128,1536]{2,1,0:T(8,128)(2,1)}, f32[2,128,1536]{2,1,0:T(8,128)}, f32...) custom-call(s32[2]{0:T(128)} %copy-done.69, ...), custom_call_target="tpu_custom_call" | custom-call | flops 1 | bytes 1 | tf_op jit(solution)/shard_map/ffn/pallas_call | solution.py:465
  291.9 5.6 collective-permute-done.46
  314.2 6.6 %collective-permute-done.48 = bf16[128,1536]{1,0:T(8,128)(2,1)S(1)} collective-permute-done((bf16[128,1536]{1,0:T(8,128)(2,1)S(1)}, bf16[128,1536]{1,0:T(8,128)(2,1)S(1)}, u32[]{:S(2)}, u32[]{:S(2)}) %collective-permute-start.48) | collective-permute-done | bytes 393248 | tf_op jit(solution)/shard_map/ppermute | solution.py:554
  328.5 7.1 %collective-permute-done.50 = bf16[128,1536]{1,0:T(8,128)(2,1)} collective-permute-done((bf16[128,1536]{1,0:T(8,128)(2,1)}, bf16[128,1536]{1,0:T(8,128)(2,1)}, u32[]{:S(2)}, u32[]{:S(2)}) %collective-permute-start.50) | collective-permute-done | bytes 393248 | tf_op jit(solution)/shard_map/ppermute | solution.py:554
  353.2 6.8 %dot_split.3 = (bf16[2,128,1536]{2,1,0:T(8,128)(2,1)S(1)}, bf16[2,128,1536]{2,1,0:T(8,128)(2,1)S(1)}, f32[2,128,1536]{2,1,0:T(8,128)S(1)}, f32[2,128,1536]{2,1,0:T(8,128)}) custom-call(bf16[1024,1024]{1,0:T(8,128)(2,1)} %get-tuple-element.302.refs_0_, bf16[1024,1536]{1,0:T(8,128)(2,1)} %assemble.1.refs_1_), custom_call_target="tpu_custom_call" | custom-call | flops 1 | bytes 1 | tf_op jit(solution)/shard_map/dot_split/pallas_call | solution.py:379
  360.1 8.0 %collective-permute-done.55 = bf16[192,2048]{1,0:T(8,128)(2,1)S(1)} collective-permute-done((bf16[192,2048]{1,0:T(8,128)(2,1)S(1)}, bf16[192,2048]{1,0:T(8,128)(2,1)S(1)}, u32[]{:S(2)}, u32[]{:S(2)}) %collective-permute-start.55) | collective-permute-done | bytes 786464 | tf_op jit(solution)/shard_map/ppermute | solution.py:564
  445.8 7.5 %attend_back.14 = (f32[2,128,1024]{2,1,0:T(8,128)}, bf16[512,384]{1,0:T(8,128)(2,1)S(1)}, bf16[512,384]{1,0:T(8,128)(2,1)S(1)}) custom-call(s32[4]{0:T(128)S(1)} %pad_add_fusion.refs_0_, bf16[1024,512]{1,0:T(8,128)(2,1)} %get-tuple-element.207.refs_1_, bf16[1024,384]{1,0:T(8,128)(2,1)S(1)} %copy-done.2, ...), custom_call_target="tpu_custom_call", output_to_operand_aliasing={{0}: (12, {})} | custom-call | flops 1 | bytes 6000000 | tf_op jit(solution)/shard_map/attend_back/pallas_call | solution.py:183
  453.4 5.6 collective-permute-done.62.refs_13_
  458.9 7.4 %attend_back.15 = (f32[2,128,1024]{2,1,0:T(8,128)}, bf16[512,384]{1,0:T(8,128)(2,1)S(1)}, bf16[512,384]{1,0:T(8,128)(2,1)S(1)}) custom-call(s32[4]{0:T(128)S(1)} %pad_add_fusion.refs_0_, bf16[1024,512]{1,0:T(8,128)(2,1)} %get-tuple-element.207.refs_1_, bf16[1024,384]{1,0:T(8,128)(2,1)S(1)} %copy-done.2, ...), custom_call_target="tpu_custom_call", output_to_operand_aliasing={{0}: (12, {})} | custom-call | flops 1 | bytes 6000000 | tf_op jit(solution)/shard_map/attend_back/pallas_call | solution.py:183
  467.7 11.4 %project_back.1 = (bf16[2,128,1536]{2,1,0:T(8,128)(2,1)S(1)}, bf16[2,128,1536]{2,1,0:T(8,128)(2,1)S(1)}, f32[2,128,1536]{2,1,0:T(8,128)}, f32[2,128,1536]{2,1,0:...) custom-call(s32[2]{0:T(128)S(1)} %copy-done.71, ...), custom_call_target="tpu_custom_call" | custom-call | flops 1 | bytes 1 | tf_op jit(solution)/shard_map/project_back/pallas_call | solution.py:527
  489.9 7.2 %collective-permute-start.74 = (bf16[192,1280]{1,0:T(8,128)(2,1)S(1)}, bf16[192,1280]{1,0:T(8,128)(2,1)S(1)}, u32[]{:S(2)}, u32[]{:S(2)}) collective-permute-start(bf16[192,1280]{1,0:T(8,128)(2,1)S(1)} %dynamic-slice_bitcast_fusion.2), channel_id=1, source_target_pairs={{0,12},{4,0},{8,4},{12,8},{1,13},{5,1},{9,5},{13,9},{2,14},{6,2},{... | collective-permute-start | bytes 1474568 | tf_op jit(solution)/shard_map/ppermute | solution.py:564
  509.4 8.5 %collective-permute-start.77 = (bf16[192,1280]{1,0:T(8,128)(2,1)S(1)}, bf16[192,1280]{1,0:T(8,128)(2,1)S(1)}, u32[]{:S(2)}, u32[]{:S(2)}) collective-permute-start(bf16[192,1280]{1,0:T(8,128)(2,1)S(1)} %fusion.18), channel_id=1, source_target_pairs={{0,12},{4,0},{8,4},{12,8},{1,13},{5,1},{9,5},{13,9},{2,14},{6,2},{... | collective-permute-start | bytes 1474568 | tf_op jit(solution)/shard_map/ppermute | solution.py:564
  525.2 5.8 %collective-permute-done.76 = bf16[128,1536]{1,0:T(8,128)(2,1)} collective-permute-done((bf16[128,1536]{1,0:T(8,128)(2,1)}, bf16[128,1536]{1,0:T(8,128)(2,1)}, u32[]{:S(2)}, u32[]{:S(2)}) %collective-permute-start.76) | collective-permute-done | bytes 393248 | tf_op jit(solution)/shard_map/ppermute | solution.py:554
  (632 shorter events, 340.6 us)
Async XLA Ops:
  39.9 28.4 %collective-permute-start.7 = (bf16[192,1280]{1,0:T(8,128)(2,1)S(1)}, bf16[192,1280]{1,0:T(8,128)(2,1)S(1)}, u32[]{:S(2)}, u32[]{:S(2)}) collective-permute-start(bf16[192,1280]{1,0:T(8,128)(2,1)S(1)} %bitcast.308), channel_id=1, source_target_pairs={{0,16},{16,0},{1,17},{17,1},{2,18},{18,2},{3,19},{19,3},{4,20},{20... | collective-permute-start | bytes 1474568 | tf_op jit(solution)/shard_map/ppermute | solution.py:558
  41.0 27.2 %all-to-all-start.1 = ((bf16[48,4,2048]{2,0,1:T(8,128)(2,1)}), bf16[48,4,2048]{2,0,1:T(8,128)(2,1)}, u32[]{:S(2)}, u32[]{:S(2)}) async-start(bf16[48,4,2048]{2,0,1:T(8,128)(2,1)} %bitcast.300), calls=%async_computation.1 | async-start | bytes 1572864 | tf_op jit(solution)/shard_map/all_to_all | solution.py:628
  68.1 39.3 %collective-permute-start.13 = (bf16[192,2048]{1,0:T(8,128)(2,1)}, bf16[192,2048]{1,0:T(8,128)(2,1)}, u32[]{:S(2)}, u32[]{:S(2)}) collective-permute-start(bf16[192,2048]{1,0:T(8,128)(2,1)} %bitcast.22.refs_3_), channel_id=1, source_target_pairs={{0,4},{4,8},{8,12},{12,0},{1,5},{5,9},{9,13},{13,1},{2,6},{6,10},{... | collective-permute-start | bytes 2359304 | tf_op jit(solution)/shard_map/ppermute | solution.py:564
  82.8 24.6 %collective-permute-start.15 = (bf16[128,1536]{1,0:T(8,128)(2,1)}, bf16[128,1536]{1,0:T(8,128)(2,1)}, u32[]{:S(2)}, u32[]{:S(2)}) collective-permute-start(bf16[128,1536]{1,0:T(8,128)(2,1)} %get-tuple-element.225), channel_id=1, source_target_pairs={{0,2},{1,3},{2,0},{3,1},{4,6},{5,7},{6,4},{7,5},{8,10},{9,11},{10,... | collective-permute-start | bytes 1179656 | tf_op jit(solution)/shard_map/ppermute | solution.py:554
  84.5 23.0 %collective-permute-start.14 = (bf16[128,1536]{1,0:T(8,128)(2,1)}, bf16[128,1536]{1,0:T(8,128)(2,1)}, u32[]{:S(2)}, u32[]{:S(2)}) collective-permute-start(bf16[128,1536]{1,0:T(8,128)(2,1)} %get-tuple-element.223), channel_id=1, source_target_pairs={{0,1},{1,0},{2,3},{3,2},{4,5},{5,4},{6,7},{7,6},{8,9},{9,8},{10,11... | collective-permute-start | bytes 1179656 | tf_op jit(solution)/shard_map/ppermute | solution.py:554
  86.9 20.6 %collective-permute-start.12 = (bf16[512,384]{1,0:T(8,128)(2,1)}, bf16[512,384]{1,0:T(8,128)(2,1)}, u32[]{:S(2)}, u32[]{:S(2)}) collective-permute-start(bf16[512,384]{1,0:T(8,128)(2,1)} %get-tuple-element.416), channel_id=1, source_target_pairs={{0,4},{4,8},{8,12},{1,5},{5,9},{9,13},{2,6},{6,10},{10,14},{3,7},{... | collective-permute-start | bytes 1179656 | tf_op jit(solution)/shard_map/ppermute | solution.py:564
  103.1 23.8 %all-to-all-start.2 = ((bf16[4,384,384]{2,1,0:T(8,128)(2,1)}), bf16[4,384,384]{2,1,0:T(8,128)(2,1)}, u32[]{:S(2)}, u32[]{:S(2)}) async-start(bf16[4,384,384]{2,1,0:T(8,128)(2,1)} %bitcast.354), calls=%async_computation.2 | async-start | bytes 2359296 | tf_op jit(solution)/shard_map/all_to_all | solution.py:628
  109.7 29.3 %collective-permute-start.19 = (bf16[2,128,1536]{2,1,0:T(8,128)(2,1)}, bf16[2,128,1536]{2,1,0:T(8,128)(2,1)}, u32[]{:S(2)}, u32[]{:S(2)}) collective-permute-start(bf16[2,128,1536]{2,1,0:T(8,128)(2,1)} %pad_maximum_fusion.6), channel_id=1, source_target_pairs={{0,1},{1,0},{2,3},{3,2},{4,5},{5,4},{6,7},{7,6},{8,9},{9,8},{10,11... | collective-permute-start | bytes 2359304 | tf_op jit(solution)/shard_map/ppermute | solution.py:554
  113.7 25.3 %collective-permute-start.18 = (bf16[2,128,1536]{2,1,0:T(8,128)(2,1)}, bf16[2,128,1536]{2,1,0:T(8,128)(2,1)}, u32[]{:S(2)}, u32[]{:S(2)}) collective-permute-start(bf16[2,128,1536]{2,1,0:T(8,128)(2,1)} %pad_maximum_fusion.5), channel_id=1, source_target_pairs={{0,2},{1,3},{2,0},{3,1},{4,6},{5,7},{6,4},{7,5},{8,10},{9,11},{10,... | collective-permute-start | bytes 2359304 | tf_op jit(solution)/shard_map/ppermute | solution.py:554
  161.2 81.6 %collective-permute-start.35 = (bf16[192,2048]{1,0:T(8,128)(2,1)}, bf16[192,2048]{1,0:T(8,128)(2,1)S(1)}, u32[]{:S(2)}, u32[]{:S(2)}) collective-permute-start(bf16[192,2048]{1,0:T(8,128)(2,1)} %bitcast.22.refs_3_), channel_id=1, source_target_pairs={{0,16},{16,0},{1,17},{17,1},{2,18},{18,2},{3,19},{19,3},{4,20},{20... | collective-permute-start | bytes 2359304 | tf_op jit(solution)/shard_map/ppermute | solution.py:558
  171.6 22.6 %collective-permute-start.25 = (bf16[192,2048]{1,0:T(8,128)(2,1)}, bf16[192,2048]{1,0:T(8,128)(2,1)S(1)}, u32[]{:S(2)}, u32[]{:S(2)}) collective-permute-start(bf16[192,2048]{1,0:T(8,128)(2,1)} %collective-permute-done.13.refs_4_), channel_id=1, source_target_pairs={{0,4},{4,8},{8,12},{12,0},{1,5},{5,9},{9,13},{13,1},{2,6},{6,10},{... | collective-permute-start | bytes 2359304 | tf_op jit(solution)/shard_map/ppermute | solution.py:564
  171.9 22.3 %collective-permute-start.23 = (bf16[2,128,1536]{2,1,0:T(8,128)(2,1)S(1)}, bf16[2,128,1536]{2,1,0:T(8,128)(2,1)S(1)}, u32[]{:S(2)}, u32[]{:S(2)}) collective-permute-start(bf16[2,128,1536]{2,1,0:T(8,128)(2,1)S(1)} %get-tuple-element.251), channel_id=1, source_target_pairs={{0,1},{1,0},{2,3},{3,2},{4,5},{5,4},{6,7},{7,6},{8,9},{9,8},{10,11... | collective-permute-start | bytes 2359304 | tf_op jit(solution)/shard_map/ppermute | solution.py:554
  173.6 20.5 %collective-permute-start.24 = (bf16[2,128,1536]{2,1,0:T(8,128)(2,1)S(1)}, bf16[2,128,1536]{2,1,0:T(8,128)(2,1)S(1)}, u32[]{:S(2)}, u32[]{:S(2)}) collective-permute-start(bf16[2,128,1536]{2,1,0:T(8,128)(2,1)S(1)} %get-tuple-element.252), channel_id=1, source_target_pairs={{0,2},{1,3},{2,0},{3,1},{4,6},{5,7},{6,4},{7,5},{8,10},{9,11},{10,... | collective-permute-start | bytes 2359304 | tf_op jit(solution)/shard_map/ppermute | solution.py:554
  314.0 25.6 %collective-permute-start.51 = (bf16[192,2048]{1,0:T(8,128)(2,1)}, bf16[192,2048]{1,0:T(8,128)(2,1)}, u32[]{:S(2)}, u32[]{:S(2)}) collective-permute-start(bf16[192,2048]{1,0:T(8,128)(2,1)} %dynamic-slice_bitcast_fusion), channel_id=1, source_target_pairs={{0,12},{4,0},{8,4},{12,8},{1,13},{5,1},{9,5},{13,9},{2,14},{6,2},{... | collective-permute-start | bytes 2359304 | tf_op jit(solution)/shard_map/ppermute | solution.py:564
  345.2 22.9 %collective-permute-start.55 = (bf16[192,2048]{1,0:T(8,128)(2,1)S(1)}, bf16[192,2048]{1,0:T(8,128)(2,1)S(1)}, u32[]{:S(2)}, u32[]{:S(2)}) collective-permute-start(bf16[192,2048]{1,0:T(8,128)(2,1)S(1)} %fusion.14), channel_id=1, source_target_pairs={{0,12},{4,0},{8,4},{12,8},{1,13},{5,1},{9,5},{13,9},{2,14},{6,2},{... | collective-permute-start | bytes 2359304 | tf_op jit(solution)/shard_map/ppermute | solution.py:564
  346.7 23.7 %collective-permute-start.54 = (bf16[2,128,1536]{2,1,0:T(8,128)(2,1)S(1)}, bf16[2,128,1536]{2,1,0:T(8,128)(2,1)S(1)}, u32[]{:S(2)}, u32[]{:S(2)}) collective-permute-start(bf16[2,128,1536]{2,1,0:T(8,128)(2,1)S(1)} %pad_maximum_fusion.10), channel_id=1, source_target_pairs={{0,1},{1,0},{2,3},{3,2},{4,5},{5,4},{6,7},{7,6},{8,9},{9,8},{10,11... | collective-permute-start | bytes 2359304 | tf_op jit(solution)/shard_map/ppermute | solution.py:554
  348.7 21.7 %collective-permute-start.53 = (bf16[2,128,1536]{2,1,0:T(8,128)(2,1)S(1)}, bf16[2,128,1536]{2,1,0:T(8,128)(2,1)S(1)}, u32[]{:S(2)}, u32[]{:S(2)}) collective-permute-start(bf16[2,128,1536]{2,1,0:T(8,128)(2,1)S(1)} %pad_maximum_fusion.9), channel_id=1, source_target_pairs={{0,2},{1,3},{2,0},{3,1},{4,6},{5,7},{6,4},{7,5},{8,10},{9,11},{10,... | collective-permute-start | bytes 2359304 | tf_op jit(solution)/shard_map/ppermute | solution.py:554
  374.8 28.3 %collective-permute-start.67 = (bf16[192,2048]{1,0:T(8,128)(2,1)}, bf16[192,2048]{1,0:T(8,128)(2,1)}, u32[]{:S(2)}, u32[]{:S(2)}) collective-permute-start(bf16[192,2048]{1,0:T(8,128)(2,1)} %fusion.13), channel_id=1, source_target_pairs={{0,12},{4,0},{8,4},{12,8},{1,13},{5,1},{9,5},{13,9},{2,14},{6,2},{... | collective-permute-start | bytes 2359304 | tf_op jit(solution)/shard_map/ppermute | solution.py:564
  392.6 39.1 %all-to-all-start.3 = ((bf16[384,4,384]{2,0,1:T(8,128)(2,1)}), bf16[384,4,384]{2,0,1:T(8,128)(2,1)}, u32[]{:S(2)}, u32[]{:S(2)}) async-start(bf16[384,4,384]{2,0,1:T(8,128)(2,1)} %bitcast.338), calls=%async_computation.3 | async-start | bytes 2359296 | tf_op jit(solution)/shard_map/all_to_all | solution.py:628
  399.6 32.0 %collective-permute-start.60 = (bf16[2,128,1536]{2,1,0:T(8,128)(2,1)}, bf16[2,128,1536]{2,1,0:T(8,128)(2,1)}, u32[]{:S(2)}, u32[]{:S(2)}) collective-permute-start(bf16[2,128,1536]{2,1,0:T(8,128)(2,1)} %copy-done.74), channel_id=1, source_target_pairs={{0,1},{1,0},{2,3},{3,2},{4,5},{5,4},{6,7},{7,6},{8,9},{9,8},{10,11... | collective-permute-start | bytes 2359304 | tf_op jit(solution)/shard_map/ppermute | solution.py:554
  401.6 30.0 %collective-permute-start.61 = (bf16[2,128,1536]{2,1,0:T(8,128)(2,1)}, bf16[2,128,1536]{2,1,0:T(8,128)(2,1)}, u32[]{:S(2)}, u32[]{:S(2)}) collective-permute-start(bf16[2,128,1536]{2,1,0:T(8,128)(2,1)} %copy-done.73), channel_id=1, source_target_pairs={{0,2},{1,3},{2,0},{3,1},{4,6},{5,7},{6,4},{7,5},{8,10},{9,11},{10,... | collective-permute-start | bytes 2359304 | tf_op jit(solution)/shard_map/ppermute | solution.py:554
  432.9 26.0 %collective-permute-start.63 = (bf16[4,192,384]{2,1,0:T(8,128)(2,1)S(1)}, bf16[4,192,384]{2,1,0:T(8,128)(2,1)S(1)}, u32[]{:S(2)}, u32[]{:S(2)}) collective-permute-start(bf16[4,192,384]{2,1,0:T(8,128)(2,1)S(1)} %dynamic-slice_bitcast_fusion.1), channel_id=1, source_target_pairs={{0,16},{16,0},{1,17},{17,1},{2,18},{18,2},{3,19},{19,3},{4,20},{20... | collective-permute-start | bytes 1769480 | tf_op jit(solution)/shard_map/ppermute | solution.py:558
  498.4 25.6 %all-to-all-start.4 = ((bf16[4,48,2048]{2,1,0:T(8,128)(2,1)}), bf16[4,48,2048]{2,1,0:T(8,128)(2,1)}, u32[]{:S(2)}, u32[]{:S(2)}) async-start(bf16[4,48,2048]{2,1,0:T(8,128)(2,1)} %bitcast.340), calls=%async_computation.4 | async-start | bytes 1572864 | tf_op jit(solution)/shard_map/all_to_all | solution.py:628
  509.4 21.6 %collective-permute-start.77 = (bf16[192,1280]{1,0:T(8,128)(2,1)S(1)}, bf16[192,1280]{1,0:T(8,128)(2,1)S(1)}, u32[]{:S(2)}, u32[]{:S(2)}) collective-permute-start(bf16[192,1280]{1,0:T(8,128)(2,1)S(1)} %fusion.18), channel_id=1, source_target_pairs={{0,12},{4,0},{8,4},{12,8},{1,13},{5,1},{9,5},{13,9},{2,14},{6,2},{... | collective-permute-start | bytes 1474568 | tf_op jit(solution)/shard_map/ppermute | solution.py:564
  (210 other events, 2105.3 us)
where the time goes:
time: 575 us; the launch traced here: 565 us
  waiting for transfers between devices  156 us (27%)
  Pallas kernels  128 us (22%)
  starting transfers between devices  126 us (22%)
  local copies, waits for them, and re-layouts  74.4 us (13%)
  other arithmetic  73 us (13%)
    ppermute x30, waiting for transfers between devices, along(): return lax.ppermute(value, 'zed', pairs)  84.5 us
    ppermute x30, starting transfers between devices, along(): return lax.ppermute(value, 'zed', pairs)  58.8 us
    ppermute x32, waiting for transfers between devices, beside(): return lax.ppermute(value, 'plane', [(i, i ^ bit) for i in range(PLANE)])  53.5 us
    pallas_call x16, Pallas kernels, run_kernel(): pl.pallas_call(body, grid_spec=pltpu.PrefetchScalarGridSpec(num_scalar_pr...  49.7 us
    pallas_call x1, Pallas kernels, ffn(): pl.pallas_call(lambda *refs: ffn_kernel(size, tok_rows, *refs), grid_spec...  41 us
    ppermute x32, starting transfers between devices, beside(): return lax.ppermute(value, 'plane', [(i, i ^ bit) for i in range(PLANE)])  35.2 us
    unnamed x324, local copies, waits for them, and re-layouts  27.2 us
    all_to_all x6, starting transfers between devices, plane_swap(): lax.all_to_all(value, 'plane', split_axis=split, concat_axis=concat, tile...  25.7 us
  transfers between devices with their start and end apart: 85, of which 39 were waited for; matrix products, arithmetic and copies ran while one was open for 21% of the time, Pallas kernels for 12%

commit v1 on v0

--- a/solution.py
+++ b/solution.py
@@ -55,8 +55,17 @@
     return lax.dot_general(a, b, (((0,), (0,)), ((), ())), preferred_element_type=f32)
 
 
-def project_kernel(size, info_ref, x_ref, cos_ref, sin_ref, e4_ref, e8_ref, *rest):
-    blocks, (n_ref, q_ref, kv_ref, w_ref, out_w_ref, gains_ref, scale_ref, pad_s) = rest[: 2 * size], rest[2 * size :]
+def piece_halves(one_ref, one_more_ref, two_ref, two_more_ref):
+    return [
+        [(one_ref, 0), (one_ref, 1)],
+        [(one_more_ref, 0), (one_more_ref, 1)],
+        [(two_ref, 0), (two_more_ref, 0)],
+        [(two_ref, 1), (two_more_ref, 1)],
+    ]
+
+
+def project_kernel(size, info_ref, one_ref, two_ref, one_more_ref, two_more_ref, cos_ref, sin_ref, e4_ref, e8_ref, *rest):
+    blocks, (x_ref, n_ref, q_ref, kv_ref, w_ref, out_w_ref, gains_ref, scale_ref, pad_s) = rest[: 2 * size], rest[2 * size :]
     rows = blocks[0].shape[0]
     heads = 8 * DH
 
@@ -71,6 +80,14 @@
         rows_to = lax.broadcasted_iota(jnp.int32, (LANES, LANES), 0)
         same = (rows_to == lax.broadcasted_iota(jnp.int32, (LANES, LANES), 1)).astype(bf16)
         gains_ref[...] = dot_nt(same[:8], w_ref[:, heads:])
+
+    tok_rows = one_ref.shape[1]
+    for i, halves in enumerate(piece_halves(one_ref, one_more_ref, two_ref, two_more_ref)):
+
+        @pl.when(pl.program_id(0) == i)
+        def _(halves=halves):
+            for j, (ref, slot) in enumerate(halves):
+                x_ref[j * tok_rows : (j + 1) * tok_rows, :] = ref[slot]
 
     x = x_ref[...].astype(f32)
     scale = rms_scale(x)
@@ -89,9 +106,9 @@
     kv_ref[...] = dot_nt(jnp.concatenate(parts[4:], axis=1), e4_ref[...]).astype(bf16)
 
 
-def project(info, x, blocks, cos, sin, e4, e8):
-    rows, width = x.shape
-    step = min(256, rows)
+def project(info, pieces, blocks, cos, sin, e4, e8):
+    _, tok_rows, width = pieces[0].shape
+    rows, step = 2 * PLANE * tok_rows, 2 * tok_rows
     size = len(blocks) // 2
     cols = blocks[0].shape[1]
     first = 8 * DH + LANES
@@ -102,8 +119,11 @@
         grid_spec=pltpu.PrefetchScalarGridSpec(
             num_scalar_prefetch=1,
             grid=(rows // step,),
-            in_specs=[by_row(width), by_row(LANES), by_row(LANES), whole(e4), whole(e8)] + [whole(b) for b in blocks],
+            in_specs=[whole(a) for a in pieces]
+            + [by_row(LANES), by_row(LANES), whole(e4), whole(e8)]
+            + [whole(b) for b in blocks],
             out_specs=[
+                by_row(width),
                 by_row(width),
                 by_row(4 * LANES),
                 by_row(4 * DH),
@@ -116,6 +136,7 @@
         ),
         out_shape=[
             jax.ShapeDtypeStruct((rows, width), bf16),
+            jax.ShapeDtypeStruct((rows, width), bf16),
             jax.ShapeDtypeStruct((rows, 4 * LANES), bf16),
             jax.ShapeDtypeStruct((rows, 4 * DH), bf16),
             jax.ShapeDtypeStruct((width, first), bf16),
@@ -126,7 +147,7 @@
         compiler_params=pltpu.CompilerParams(vmem_limit_bytes=VMEM_BYTES),
         cost_estimate=LIGHT,
         name="project",
-    )(info, x, cos, sin, e4, e8, *blocks)
+    )(info, *pieces, cos, sin, e4, e8, *blocks)
 
 
 def assemble_kernel(size, info_ref, *rest):
@@ -390,11 +411,11 @@
     )
 
 
-def ffn_kernel(size, tok_rows, info_ref, n_ref, g_ref, *rest):
+def ffn_kernel(size, tok_rows, info_ref, one_ref, two_ref, one_more_ref, two_more_ref, g_ref, *rest):
     gu_blocks, down_blocks, rest = rest[: 2 * size], rest[2 * size : 4 * size], rest[4 * size :]
     hidden_ref, *outs = rest[:5]
     gu_theirs_ref, gu_mine_ref, down_theirs_ref, down_mine_ref = rest[5:9]
-    gu_s, down_s, acc_s, flat_s, grad_s = rest[9:]
+    gu_s, down_s, acc_s, flat_s, grad_s, n_ref, sems = rest[9:]
     f, last = pl.program_id(0), pl.num_programs(0) - 1
     units = hidden_ref.shape[1]
     half = flat_s.shape[0] // 2
@@ -405,7 +426,15 @@
 
     @pl.when(f == 0)
     def _():
+        copies = []
+        for i, halves in enumerate(piece_halves(one_ref, one_more_ref, two_ref, two_more_ref)):
+            for j, (ref, slot) in enumerate(halves):
+                at = pl.ds((2 * i + j) * tok_rows, tok_rows)
+                copies.append(pltpu.make_async_copy(ref.at[slot], n_ref.at[at], sems.at[2 * i + j]))
+                copies[-1].start()
         acc_s[...] = jnp.zeros(acc_s.shape, f32)
+        for copy in copies:
+            copy.wait()
         flat_s[...] = n_ref[...].T
         for i, block in enumerate(down_blocks):
             down_s[place(i, block.shape[0]), :] = block[...]
@@ -448,8 +477,8 @@
         store_split(lambda start, n: acc_s[start : start + n, :], tok_rows, *outs)
 
 
-def ffn(info, normed, grad_mlp, gu_blocks, down_blocks):
-    rows, width = normed.shape
+def ffn(info, pieces, grad_mlp, gu_blocks, down_blocks):
+    rows, width = grad_mlp.shape
     size = len(gu_blocks) // 2
     tok_rows = rows // (2 * PLANE)
     ff_part = gu_blocks[0].shape[1] // 2
@@ -467,7 +496,8 @@
             grid_spec=pltpu.PrefetchScalarGridSpec(
                 num_scalar_prefetch=1,
                 grid=(FF_TILES,),
-                in_specs=[whole(normed), whole(grad_mlp)]
+                in_specs=[pl.BlockSpec(memory_space=pl.ANY) for _ in pieces]
+                + [whole(grad_mlp)]
                 + [pl.BlockSpec((block.shape[0], 2 * units), lambda f, n: (0, f)) for block in gu_blocks]
                 + [whole(block) for block in down_blocks],
                 out_specs=[pl.BlockSpec((rows, units), lambda f, n: (0, f))]
@@ -479,6 +509,8 @@
                     pltpu.VMEM((rows, width), f32),
                     pltpu.VMEM((width, rows), bf16),
                     pltpu.VMEM((rows, 2 * units), bf16),
+                    pltpu.VMEM((rows, width), bf16),
+                    pltpu.SemaphoreType.DMA((2 * PLANE,)),
                 ],
             ),
             out_shape=[jax.ShapeDtypeStruct((rows, ff_part), bf16)]
@@ -488,7 +520,7 @@
             compiler_params=pltpu.CompilerParams(vmem_limit_bytes=58 * 1024 * 1024),
             cost_estimate=LIGHT,
             name="ffn",
-        )(info, normed, grad_mlp, *gu_blocks, *down_blocks)
+        )(info, *pieces, grad_mlp, *gu_blocks, *down_blocks)
     )
 
 
@@ -662,10 +694,10 @@
     qkv_blocks = [qkv_block]
     for _ in range(size - 1):
         qkv_blocks.append(along(qkv_blocks[-1], 1, True))
-    qkv_other = [other_core(block) for block in qkv_blocks]
     ffn_block = plane_swap(after(ffn_bundle, qkv_block), 1, 0)
     pieces = sync(*plane_gather_start(after(own_in, qkv_block)))
-    gathered_in = plane_gather_end(*sync(*plane_gather_more(*pieces)))
+    *in_pieces, qkv_blocks[-1] = sync(*plane_gather_more(*pieces), qkv_blocks[-1])
+    qkv_other = [other_core(block) for block in qkv_blocks]
     gu_blocks = [after(ffn_block, qkv_blocks[-1])]
     gu_blocks.append(along(gu_blocks[0], 1, True))
 
@@ -697,13 +729,12 @@
     qbeg = jnp.tile(own_begin, (1, 2))[:, None]
     kpos = slot_place[:, None]
 
-    normed_one, q_rot, kv_own, full_qkv, full_oc, full_gains, in_scale = project(
-        index, gathered_in, qkv_blocks + qkv_other, cos.reshape(tokens, LANES), sin.reshape(tokens, LANES), e4, e8
-    )
-    full_qkv = full_qkv[:, : q_part + 2 * kv_part]
+    gathered_in, normed_one, q_rot, kv_own, full_qkv, full_oc, full_gains, in_scale = project(
+        index, in_pieces, qkv_blocks + qkv_other, cos.reshape(tokens, LANES), sin.reshape(tokens, LANES), e4, e8
+    )
     gain_one, gain_two = full_gains[0:1], full_gains[1:2]
     full_out = plane_swap(full_oc, 0, 1)
-    cot_pieces = plane_gather_start(after(own_cot, gathered_in, kv_own))
+    cot_pieces = plane_gather_start(after(own_cot, kv_own))
     q_rot = [(q_rot, (chunk, 4 * LANES), (m, 0)) for m in range(micro)]
     kv_windows = [[(kv_own, (chunk, 4 * DH), (m, 0))] for m in range(micro)]
     kv_pieces = [[piece] for piece in kv_own.reshape(micro, chunk, 4 * DH)]
@@ -754,11 +785,10 @@
     for k in range(2, size - 1):
         gu_blocks.append(along(after(gu_blocks[k], down_blocks[-1]), 1, True))
     *pieces, gu_blocks[-1] = sync(*plane_gather_more(*pieces), gu_blocks[-1])
-    normed_two = plane_gather_end(*pieces)
 
     gu_all = gu_blocks + [other_core(block) for block in gu_blocks]
     down_all = down_blocks + [other_core(block) for block in down_blocks]
-    hidden, *outs = ffn(index, normed_two, gathered_cot, gu_all, down_all)
+    hidden, *outs = ffn(index, pieces, gathered_cot, gu_all, down_all)
     normed_split, (gu_theirs, gu_mine, down_theirs, down_mine) = outs[:4], outs[4:]
     got = plane_sum_start(normed_split)
     gu_half = core_sum(gu_mine, other_core(gu_theirs)).reshape(size, -1, 2 * ff_part)

time: 575 us -> 565 us (0.983)
  waiting for transfers between devices: 156 us -> 142 us
  blocking collectives: 0 us -> 13.2 us
  local copies, waits for them, and re-layouts: 74.4 us -> 63.3 us
    ppermute x30, waiting for transfers between devices: 84.5 us -> 64.6 us  [along(): return lax.ppermute(value, 'zed', pairs)]
    all_to_all x0 -> x1, blocking collectives: none -> 13.2 us  [plane_swap(): lax.all_to_all(value, 'plane', split_axis=split, concat_axis=concat, tile...]
    ppermute x32, waiting for transfers between devices: 53.5 us -> 66.5 us  [beside(): return lax.ppermute(value, 'plane', [(i, i ^ bit) for i in range(PLANE)])]
    unnamed x324 -> x318, local copies, waits for them, and re-layouts: 27.2 us -> 22 us
    all_to_all x6 -> x5, starting transfers between devices: 25.7 us -> 20.5 us  [plane_swap(): lax.all_to_all(value, 'plane', split_axis=split, concat_axis=concat, tile...]
  transfers between devices with their start and end apart: 85 -> 84, of which waited for: 39 -> 38; matrix products, arithmetic and copies ran while one was open for 21% -> 20% of each run, Pallas kernels for 12% -> 13%
where the time goes in v1:
time: 565 us; the launch traced here: 555 us
  waiting for transfers between devices  142 us (25%)
  Pallas kernels  130 us (23%)
  starting transfers between devices  124 us (22%)
  other arithmetic  75.8 us (13%)
  local copies, waits for them, and re-layouts  63.3 us (11%)
  blocking collectives  13.2 us (2%)
    ppermute x32, waiting for transfers between devices, beside(): return lax.ppermute(value, 'plane', [(i, i ^ bit) for i in range(PLANE)])  66.5 us
    ppermute x30, waiting for transfers between devices, along(): return lax.ppermute(value, 'zed', pairs)  64.6 us
    ppermute x30, starting transfers between devices, along(): return lax.ppermute(value, 'zed', pairs)  63.2 us
    pallas_call x16, Pallas kernels, run_kernel(): pl.pallas_call(body, grid_spec=pltpu.PrefetchScalarGridSpec(num_scalar_pr...  49.2 us
    pallas_call x1, Pallas kernels, ffn(): pl.pallas_call(lambda *refs: ffn_kernel(size, tok_rows, *refs), grid_spec...  41.7 us
    ppermute x32, starting transfers between devices, beside(): return lax.ppermute(value, 'plane', [(i, i ^ bit) for i in range(PLANE)])  37.2 us
    unnamed x318, local copies, waits for them, and re-layouts  22 us
    all_to_all x5, starting transfers between devices, plane_swap(): lax.all_to_all(value, 'plane', split_axis=split, concat_axis=concat, tile...  20.5 us
  transfers between devices with their start and end apart: 84, of which 38 were waited for; matrix products, arithmetic and copies ran while one was open for 20% of the time, Pallas kernels for 13%

profile of v1, /device:TPU:0, one launch (start us, length us, event | category | flops | bytes accessed | tf_op | source)
XLA Modules:
  0.0 555.0 jit_solution(5255161481973897881)
XLA Ops:
  4.8 13.2 %all_to_all.105 = bf16[48,4,1280]{2,0,1:T(8,128)(2,1)S(1)} all-to-all(bf16[48,4,1280]{2,0,1:T(8,128)(2,1)S(1)} %concatenate.46), channel_id=1, replica_groups=mesh['stream'=2,'zed'=4,'plane'=4] {'plane'}, dimensions={1} | all-to-all | bytes 983040 | tf_op jit(solution)/shard_map/all_to_all | solution.py:660
  38.6 5.2 collective-permute-done.5.refs_11_
  50.0 5.3 collective-permute-done.2.refs_3_
  63.6 14.9 %project.1 = (bf16[1024,1536]{1,0:T(8,128)(2,1)}, bf16[1024,1536]{1,0:T(8,128)(2,1)}, bf16[1024,512]{1,0:T(8,128)(2,1)}, bf16[1024,384]{1,0:T(8,128)(2,1)}, bf16...) custom-call(s32[2]{0:T(128)S(1)} %pad_add_fusion.1.refs_0_, ...), custom_call_target="tpu_custom_call" | custom-call | flops 1 | bytes 1 | tf_op jit(solution)/shard_map/project/pallas_call | solution.py:117
  129.2 6.3 %collective-permute-done.18 = bf16[2,128,1536]{2,1,0:T(8,128)(2,1)} collective-permute-done((bf16[2,128,1536]{2,1,0:T(8,128)(2,1)}, bf16[2,128,1536]{2,1,0:T(8,128)(2,1)}, u32[]{:S(2)}, u32[]{:S(2)}) %collective-permute-start.18) | collective-permute-done | bytes 786464 | tf_op jit(solution)/shard_map/ppermute | solution.py:586
  147.3 6.4 %collective-permute-done.21.refs_2_ = bf16[512,384]{1,0:T(8,128)(2,1)S(1)} collective-permute-done((bf16[512,384]{1,0:T(8,128)(2,1)}, bf16[512,384]{1,0:T(8,128)(2,1)S(1)}, u32[]{:S(2)}, u32[]{:S(2)}) %collective-permute-start.21) | collective-permute-done | bytes 393248 | tf_op jit(solution)/shard_map/ppermute | solution.py:596
  168.5 14.2 %collective-permute-done.23 = bf16[2,128,1536]{2,1,0:T(8,128)(2,1)S(1)} collective-permute-done((bf16[2,128,1536]{2,1,0:T(8,128)(2,1)S(1)}, bf16[2,128,1536]{2,1,0:T(8,128)(2,1)S(1)}, u32[]{:S(2)}, u32[]{:S(2)}) %collective-permute-start.23) | collective-permute-done | bytes 786464 | tf_op jit(solution)/shard_map/ppermute | solution.py:586
  189.3 8.9 %fusion.1 = (f32[2,4,512,128]{3,2,1,0:T(8,128)}, f32[2,4,512,128]{3,2,1,0:T(8,128)}) fusion(f32[128]{0:T(128)S(1)} %copy-done.145, f32[128]{0:T(128)S(1)} %copy-done.147, f32[2,4,512]{2,1,0:T(4,128)S(1)} %broadcast_maximum_fusion, pred[128]{0:T(512)(128)(4,1)S(1)} %copy-done.149), kind=kLoop, calls=%fused_computation.10 | loop fusion | flops 1572864 | bytes 4211840 | tf_op jit(solution)/shard_map/mul | solution.py:723
  205.0 4.7 collective-permute-done.29
  219.3 7.6 %collective-permute-done.32.refs_3_ = bf16[2,128,1536]{2,1,0:T(8,128)(2,1)S(1)} collective-permute-done((bf16[2,128,1536]{2,1,0:T(8,128)(2,1)S(1)}, bf16[2,128,1536]{2,1,0:T(8,128)(2,1)S(1)}, u32[]{:S(2)}, u32[]{:S(2)}) %collective-permute-start.32) | collective-permute-done | bytes 786464 | tf_op jit(solution)/shard_map/ppermute | solution.py:586
  236.7 41.7 %ffn.1 = (bf16[1024,1024]{1,0:T(8,128)(2,1)}, bf16[2,128,1536]{2,1,0:T(8,128)(2,1)}, bf16[2,128,1536]{2,1,0:T(8,128)(2,1)}, f32[2,128,1536]{2,1,0:T(8,128)}, f32...) custom-call(s32[2]{0:T(128)} %copy-done.71, ...), custom_call_target="tpu_custom_call" | custom-call | flops 1 | bytes 1 | tf_op jit(solution)/shard_map/ffn/pallas_call | solution.py:494
  280.6 6.0 %collective-permute-done.46 = bf16[512,1536]{1,0:T(8,128)(2,1)} collective-permute-done((bf16[512,1536]{1,0:T(8,128)(2,1)}, bf16[512,1536]{1,0:T(8,128)(2,1)}, u32[]{:S(2)}, u32[]{:S(2)}) %collective-permute-start.46) | collective-permute-done | bytes 1572896 | tf_op jit(solution)/shard_map/ppermute | solution.py:590
  303.5 6.0 %collective-permute-done.47 = bf16[128,1536]{1,0:T(8,128)(2,1)S(1)} collective-permute-done((bf16[128,1536]{1,0:T(8,128)(2,1)S(1)}, bf16[128,1536]{1,0:T(8,128)(2,1)S(1)}, u32[]{:S(2)}, u32[]{:S(2)}) %collective-permute-start.47) | collective-permute-done | bytes 393248 | tf_op jit(solution)/shard_map/ppermute | solution.py:586
  317.8 10.4 %collective-permute-done.52 = bf16[128,1536]{1,0:T(8,128)(2,1)} collective-permute-done((bf16[128,1536]{1,0:T(8,128)(2,1)}, bf16[128,1536]{1,0:T(8,128)(2,1)}, u32[]{:S(2)}, u32[]{:S(2)}) %collective-permute-start.52) | collective-permute-done | bytes 393248 | tf_op jit(solution)/shard_map/ppermute | solution.py:596
  342.0 6.8 %dot_split.3 = (bf16[2,128,1536]{2,1,0:T(8,128)(2,1)S(1)}, bf16[2,128,1536]{2,1,0:T(8,128)(2,1)S(1)}, f32[2,128,1536]{2,1,0:T(8,128)S(1)}, f32[2,128,1536]{2,1,0:T(8,128)}) custom-call(bf16[1024,1024]{1,0:T(8,128)(2,1)} %get-tuple-element.305.refs_0_, bf16[1024,1536]{1,0:T(8,128)(2,1)} %assemble.1.refs_1_), custom_call_target="tpu_custom_call" | custom-call | flops 1 | bytes 1 | tf_op jit(solution)/shard_map/dot_split/pallas_call | solution.py:400
  348.8 7.5 %collective-permute-done.56 = bf16[128,1536]{1,0:T(8,128)(2,1)S(1)} collective-permute-done((bf16[128,1536]{1,0:T(8,128)(2,1)S(1)}, bf16[128,1536]{1,0:T(8,128)(2,1)S(1)}, u32[]{:S(2)}, u32[]{:S(2)}) %collective-permute-start.56) | collective-permute-done | bytes 393248 | tf_op jit(solution)/shard_map/ppermute | solution.py:596
  368.2 4.7 collective-permute-done.57
  436.1 7.5 %attend_back.14 = (f32[2,128,1024]{2,1,0:T(8,128)}, bf16[512,384]{1,0:T(8,128)(2,1)S(1)}, bf16[512,384]{1,0:T(8,128)(2,1)S(1)}) custom-call(s32[4]{0:T(128)S(1)} %pad_add_fusion.refs_0_, bf16[1024,512]{1,0:T(8,128)(2,1)} %get-tuple-element.210.refs_1_, bf16[1024,384]{1,0:T(8,128)(2,1)S(1)} %copy-done.2, ...), custom_call_target="tpu_custom_call", output_to_operand_aliasing={{0}: (12, {})} | custom-call | flops 1 | bytes 6000000 | tf_op jit(solution)/shard_map/attend_back/pallas_call | solution.py:204
  444.5 7.4 %attend_back.15 = (f32[2,128,1024]{2,1,0:T(8,128)}, bf16[512,384]{1,0:T(8,128)(2,1)S(1)}, bf16[512,384]{1,0:T(8,128)(2,1)S(1)}) custom-call(s32[4]{0:T(128)S(1)} %pad_add_fusion.refs_0_, bf16[1024,512]{1,0:T(8,128)(2,1)} %get-tuple-element.210.refs_1_, bf16[1024,384]{1,0:T(8,128)(2,1)S(1)} %copy-done.2, ...), custom_call_target="tpu_custom_call", output_to_operand_aliasing={{0}: (12, {})} | custom-call | flops 1 | bytes 6000000 | tf_op jit(solution)/shard_map/attend_back/pallas_call | solution.py:204
  453.3 11.3 %project_back.1 = (bf16[2,128,1536]{2,1,0:T(8,128)(2,1)S(1)}, bf16[2,128,1536]{2,1,0:T(8,128)(2,1)S(1)}, f32[2,128,1536]{2,1,0:T(8,128)}, f32[2,128,1536]{2,1,0:...) custom-call(s32[2]{0:T(128)S(1)} %copy-done.73, ...), custom_call_target="tpu_custom_call" | custom-call | flops 1 | bytes 1 | tf_op jit(solution)/shard_map/project_back/pallas_call | solution.py:559
  473.8 14.6 %collective-permute-start.74 = (bf16[192,1280]{1,0:T(8,128)(2,1)S(1)}, bf16[192,1280]{1,0:T(8,128)(2,1)S(1)}, u32[]{:S(2)}, u32[]{:S(2)}) collective-permute-start(bf16[192,1280]{1,0:T(8,128)(2,1)S(1)} %dynamic-slice_bitcast_fusion.2), channel_id=1, source_target_pairs={{0,12},{4,0},{8,4},{12,8},{1,13},{5,1},{9,5},{13,9},{2,14},{6,2},{... | collective-permute-start | bytes 1474568 | tf_op jit(solution)/shard_map/ppermute | solution.py:596
  493.9 5.2 collective-permute-done.74
  504.9 4.3 collective-permute-start.77
  513.9 7.2 %collective-permute-done.76 = bf16[128,1536]{1,0:T(8,128)(2,1)} collective-permute-done((bf16[128,1536]{1,0:T(8,128)(2,1)}, bf16[128,1536]{1,0:T(8,128)(2,1)}, u32[]{:S(2)}, u32[]{:S(2)}) %collective-permute-start.76) | collective-permute-done | bytes 393248 | tf_op jit(solution)/shard_map/ppermute | solution.py:586
  (622 shorter events, 324.5 us)
Async XLA Ops:
  34.4 20.9 %collective-permute-start.2 = (bf16[2,128,1536]{2,1,0:T(8,128)(2,1)}, bf16[2,128,1536]{2,1,0:T(8,128)(2,1)}, u32[]{:S(2)}, u32[]{:S(2)}) collective-permute-start(bf16[2,128,1536]{2,1,0:T(8,128)(2,1)} %pad_maximum_fusion.2.refs_1_), channel_id=1, source_target_pairs={{0,2},{1,3},{2,0},{3,1},{4,6},{5,7},{6,4},{7,5},{8,10},{9,11},{10,... | collective-permute-start | bytes 2359304 | tf_op jit(solution)/shard_map/ppermute | solution.py:586
  37.1 20.8 %collective-permute-start.3 = (bf16[2,128,1536]{2,1,0:T(8,128)(2,1)}, bf16[2,128,1536]{2,1,0:T(8,128)(2,1)}, u32[]{:S(2)}, u32[]{:S(2)}) collective-permute-start(bf16[2,128,1536]{2,1,0:T(8,128)(2,1)} %pad_maximum_fusion.3.refs_2_), channel_id=1, source_target_pairs={{0,1},{1,0},{2,3},{3,2},{4,5},{5,4},{6,7},{7,6},{8,9},{9,8},{10,11... | collective-permute-start | bytes 2359304 | tf_op jit(solution)/shard_map/ppermute | solution.py:586
  62.3 43.3 %collective-permute-start.13 = (bf16[192,2048]{1,0:T(8,128)(2,1)}, bf16[192,2048]{1,0:T(8,128)(2,1)}, u32[]{:S(2)}, u32[]{:S(2)}) collective-permute-start(bf16[192,2048]{1,0:T(8,128)(2,1)} %bitcast.21.refs_6_), channel_id=1, source_target_pairs={{0,4},{4,8},{8,12},{12,0},{1,5},{5,9},{9,13},{13,1},{2,6},{6,10},{... | collective-permute-start | bytes 2359304 | tf_op jit(solution)/shard_map/ppermute | solution.py:596
  81.4 24.2 %collective-permute-start.11 = (bf16[512,384]{1,0:T(8,128)(2,1)}, bf16[512,384]{1,0:T(8,128)(2,1)}, u32[]{:S(2)}, u32[]{:S(2)}) collective-permute-start(bf16[512,384]{1,0:T(8,128)(2,1)} %get-tuple-element.421), channel_id=1, source_target_pairs={{0,4},{4,8},{8,12},{1,5},{5,9},{9,13},{2,6},{6,10},{10,14},{3,7},{... | collective-permute-start | bytes 1179656 | tf_op jit(solution)/shard_map/ppermute | solution.py:596
  85.4 20.3 %collective-permute-start.12 = (bf16[512,384]{1,0:T(8,128)(2,1)}, bf16[512,384]{1,0:T(8,128)(2,1)}, u32[]{:S(2)}, u32[]{:S(2)}) collective-permute-start(bf16[512,384]{1,0:T(8,128)(2,1)} %get-tuple-element.420), channel_id=1, source_target_pairs={{0,4},{4,8},{8,12},{1,5},{5,9},{9,13},{2,6},{6,10},{10,14},{3,7},{... | collective-permute-start | bytes 1179656 | tf_op jit(solution)/shard_map/ppermute | solution.py:596
  101.3 22.0 %all-to-all-start.2 = ((bf16[4,384,384]{2,1,0:T(8,128)(2,1)}), bf16[4,384,384]{2,1,0:T(8,128)(2,1)}, u32[]{:S(2)}, u32[]{:S(2)}) async-start(bf16[4,384,384]{2,1,0:T(8,128)(2,1)} %bitcast.349), calls=%async_computation.2 | async-start | bytes 2359296 | tf_op jit(solution)/shard_map/all_to_all | solution.py:660
  107.8 27.7 %collective-permute-start.18 = (bf16[2,128,1536]{2,1,0:T(8,128)(2,1)}, bf16[2,128,1536]{2,1,0:T(8,128)(2,1)}, u32[]{:S(2)}, u32[]{:S(2)}) collective-permute-start(bf16[2,128,1536]{2,1,0:T(8,128)(2,1)} %pad_maximum_fusion.5), channel_id=1, source_target_pairs={{0,2},{1,3},{2,0},{3,1},{4,6},{5,7},{6,4},{7,5},{8,10},{9,11},{10,... | collective-permute-start | bytes 2359304 | tf_op jit(solution)/shard_map/ppermute | solution.py:586
  111.9 23.7 %collective-permute-start.19 = (bf16[2,128,1536]{2,1,0:T(8,128)(2,1)}, bf16[2,128,1536]{2,1,0:T(8,128)(2,1)}, u32[]{:S(2)}, u32[]{:S(2)}) collective-permute-start(bf16[2,128,1536]{2,1,0:T(8,128)(2,1)} %pad_maximum_fusion.6), channel_id=1, source_target_pairs={{0,1},{1,0},{2,3},{3,2},{4,5},{5,4},{6,7},{7,6},{8,9},{9,8},{10,11... | collective-permute-start | bytes 2359304 | tf_op jit(solution)/shard_map/ppermute | solution.py:586
  167.0 65.0 %collective-permute-start.35 = (bf16[192,2048]{1,0:T(8,128)(2,1)}, bf16[192,2048]{1,0:T(8,128)(2,1)S(1)}, u32[]{:S(2)}, u32[]{:S(2)}) collective-permute-start(bf16[192,2048]{1,0:T(8,128)(2,1)} %bitcast.21.refs_6_), channel_id=1, source_target_pairs={{0,16},{16,0},{1,17},{17,1},{2,18},{18,2},{3,19},{19,3},{4,20},{20... | collective-permute-start | bytes 2359304 | tf_op jit(solution)/shard_map/ppermute | solution.py:590
  278.9 19.9 %collective-permute-start.43 = (bf16[2,128,1536]{2,1,0:T(8,128)(2,1)}, bf16[2,128,1536]{2,1,0:T(8,128)(2,1)S(1)}, u32[]{:S(2)}, u32[]{:S(2)}) collective-permute-start(bf16[2,128,1536]{2,1,0:T(8,128)(2,1)} %get-tuple-element.289), channel_id=1, source_target_pairs={{0,1},{1,0},{2,3},{3,2},{4,5},{5,4},{6,7},{7,6},{8,9},{9,8},{10,11... | collective-permute-start | bytes 2359304 | tf_op jit(solution)/shard_map/ppermute | solution.py:586
  301.2 27.0 %collective-permute-start.51 = (bf16[192,2048]{1,0:T(8,128)(2,1)}, bf16[192,2048]{1,0:T(8,128)(2,1)}, u32[]{:S(2)}, u32[]{:S(2)}) collective-permute-start(bf16[192,2048]{1,0:T(8,128)(2,1)} %dynamic-slice_bitcast_fusion), channel_id=1, source_target_pairs={{0,12},{4,0},{8,4},{12,8},{1,13},{5,1},{9,5},{13,9},{2,14},{6,2},{... | collective-permute-start | bytes 2359304 | tf_op jit(solution)/shard_map/ppermute | solution.py:596
  302.4 25.8 %collective-permute-start.52 = (bf16[128,1536]{1,0:T(8,128)(2,1)}, bf16[128,1536]{1,0:T(8,128)(2,1)}, u32[]{:S(2)}, u32[]{:S(2)}) collective-permute-start(bf16[128,1536]{1,0:T(8,128)(2,1)} %dynamic-slice_bitcast_fusion.3), channel_id=1, source_target_pairs={{0,12},{4,0},{8,4},{12,8},{1,13},{5,1},{9,5},{13,9},{2,14},{6,2},{... | collective-permute-start | bytes 1179656 | tf_op jit(solution)/shard_map/ppermute | solution.py:596
  330.0 26.4 %collective-permute-start.55 = (bf16[192,2048]{1,0:T(8,128)(2,1)S(1)}, bf16[192,2048]{1,0:T(8,128)(2,1)S(1)}, u32[]{:S(2)}, u32[]{:S(2)}) collective-permute-start(bf16[192,2048]{1,0:T(8,128)(2,1)S(1)} %fusion.14), channel_id=1, source_target_pairs={{0,12},{4,0},{8,4},{12,8},{1,13},{5,1},{9,5},{13,9},{2,14},{6,2},{... | collective-permute-start | bytes 2359304 | tf_op jit(solution)/shard_map/ppermute | solution.py:596
  334.1 22.2 %collective-permute-start.56 = (bf16[128,1536]{1,0:T(8,128)(2,1)S(1)}, bf16[128,1536]{1,0:T(8,128)(2,1)S(1)}, u32[]{:S(2)}, u32[]{:S(2)}) collective-permute-start(bf16[128,1536]{1,0:T(8,128)(2,1)S(1)} %fusion.23), channel_id=1, source_target_pairs={{0,12},{4,0},{8,4},{12,8},{1,13},{5,1},{9,5},{13,9},{2,14},{6,2},{... | collective-permute-start | bytes 1179656 | tf_op jit(solution)/shard_map/ppermute | solution.py:596
  335.6 23.1 %collective-permute-start.53 = (bf16[2,128,1536]{2,1,0:T(8,128)(2,1)S(1)}, bf16[2,128,1536]{2,1,0:T(8,128)(2,1)S(1)}, u32[]{:S(2)}, u32[]{:S(2)}) collective-permute-start(bf16[2,128,1536]{2,1,0:T(8,128)(2,1)S(1)} %pad_maximum_fusion.9), channel_id=1, source_target_pairs={{0,2},{1,3},{2,0},{3,1},{4,6},{5,7},{6,4},{7,5},{8,10},{9,11},{10,... | collective-permute-start | bytes 2359304 | tf_op jit(solution)/shard_map/ppermute | solution.py:586
  338.3 20.4 %collective-permute-start.54 = (bf16[2,128,1536]{2,1,0:T(8,128)(2,1)S(1)}, bf16[2,128,1536]{2,1,0:T(8,128)(2,1)S(1)}, u32[]{:S(2)}, u32[]{:S(2)}) collective-permute-start(bf16[2,128,1536]{2,1,0:T(8,128)(2,1)S(1)} %pad_maximum_fusion.10), channel_id=1, source_target_pairs={{0,1},{1,0},{2,3},{3,2},{4,5},{5,4},{6,7},{7,6},{8,9},{9,8},{10,11... | collective-permute-start | bytes 2359304 | tf_op jit(solution)/shard_map/ppermute | solution.py:586
  363.3 28.1 %collective-permute-start.67 = (bf16[192,2048]{1,0:T(8,128)(2,1)}, bf16[192,2048]{1,0:T(8,128)(2,1)}, u32[]{:S(2)}, u32[]{:S(2)}) collective-permute-start(bf16[192,2048]{1,0:T(8,128)(2,1)} %fusion.13), channel_id=1, source_target_pairs={{0,12},{4,0},{8,4},{12,8},{1,13},{5,1},{9,5},{13,9},{2,14},{6,2},{... | collective-permute-start | bytes 2359304 | tf_op jit(solution)/shard_map/ppermute | solution.py:596
  380.9 39.3 %all-to-all-start.3 = ((bf16[384,4,384]{2,0,1:T(8,128)(2,1)}), bf16[384,4,384]{2,0,1:T(8,128)(2,1)}, u32[]{:S(2)}, u32[]{:S(2)}) async-start(bf16[384,4,384]{2,0,1:T(8,128)(2,1)} %bitcast.335), calls=%async_computation.3 | async-start | bytes 2359296 | tf_op jit(solution)/shard_map/all_to_all | solution.py:660
  387.9 32.2 %collective-permute-start.60 = (bf16[2,128,1536]{2,1,0:T(8,128)(2,1)}, bf16[2,128,1536]{2,1,0:T(8,128)(2,1)}, u32[]{:S(2)}, u32[]{:S(2)}) collective-permute-start(bf16[2,128,1536]{2,1,0:T(8,128)(2,1)} %copy-done.76), channel_id=1, source_target_pairs={{0,1},{1,0},{2,3},{3,2},{4,5},{5,4},{6,7},{7,6},{8,9},{9,8},{10,11... | collective-permute-start | bytes 2359304 | tf_op jit(solution)/shard_map/ppermute | solution.py:586
  389.9 30.2 %collective-permute-start.61 = (bf16[2,128,1536]{2,1,0:T(8,128)(2,1)}, bf16[2,128,1536]{2,1,0:T(8,128)(2,1)}, u32[]{:S(2)}, u32[]{:S(2)}) collective-permute-start(bf16[2,128,1536]{2,1,0:T(8,128)(2,1)} %copy-done.75), channel_id=1, source_target_pairs={{0,2},{1,3},{2,0},{3,1},{4,6},{5,7},{6,4},{7,5},{8,10},{9,11},{10,... | collective-permute-start | bytes 2359304 | tf_op jit(solution)/shard_map/ppermute | solution.py:586
  464.6 29.3 %collective-permute-start.70 = (bf16[2,128,1536]{2,1,0:T(8,128)(2,1)S(1)}, bf16[2,128,1536]{2,1,0:T(8,128)(2,1)}, u32[]{:S(2)}, u32[]{:S(2)}) collective-permute-start(bf16[2,128,1536]{2,1,0:T(8,128)(2,1)S(1)} %get-tuple-element.370), channel_id=1, source_target_pairs={{0,1},{1,0},{2,3},{3,2},{4,5},{5,4},{6,7},{7,6},{8,9},{9,8},{10,11... | collective-permute-start | bytes 2359304 | tf_op jit(solution)/shard_map/ppermute | solution.py:586
  465.7 28.2 %collective-permute-start.71 = (bf16[2,128,1536]{2,1,0:T(8,128)(2,1)S(1)}, bf16[2,128,1536]{2,1,0:T(8,128)(2,1)}, u32[]{:S(2)}, u32[]{:S(2)}) collective-permute-start(bf16[2,128,1536]{2,1,0:T(8,128)(2,1)S(1)} %get-tuple-element.371), channel_id=1, source_target_pairs={{0,2},{1,3},{2,0},{3,1},{4,6},{5,7},{6,4},{7,5},{8,10},{9,11},{10,... | collective-permute-start | bytes 2359304 | tf_op jit(solution)/shard_map/ppermute | solution.py:586
  473.8 25.3 %collective-permute-start.74 = (bf16[192,1280]{1,0:T(8,128)(2,1)S(1)}, bf16[192,1280]{1,0:T(8,128)(2,1)S(1)}, u32[]{:S(2)}, u32[]{:S(2)}) collective-permute-start(bf16[192,1280]{1,0:T(8,128)(2,1)S(1)} %dynamic-slice_bitcast_fusion.2), channel_id=1, source_target_pairs={{0,12},{4,0},{8,4},{12,8},{1,13},{5,1},{9,5},{13,9},{2,14},{6,2},{... | collective-permute-start | bytes 1474568 | tf_op jit(solution)/shard_map/ppermute | solution.py:596
  489.7 23.0 %all-to-all-start.4 = ((bf16[4,48,2048]{2,1,0:T(8,128)(2,1)}), bf16[4,48,2048]{2,1,0:T(8,128)(2,1)}, u32[]{:S(2)}, u32[]{:S(2)}) async-start(bf16[4,48,2048]{2,1,0:T(8,128)(2,1)} %bitcast.337), calls=%async_computation.4 | async-start | bytes 1572864 | tf_op jit(solution)/shard_map/all_to_all | solution.py:660
  (211 other events, 2415.5 us)
